TPU v7x, 32 devices: a whole 2x2x4 slice. The times are simulated.
32 devices in a mesh: dp: 8 (over z, x), ctx: 2 (over core), tp: 2 (over y).
Axes of the slice: x: 2, y: 2, z: 4, core: 2. Of those that a mesh axis runs over, the one named last changes fastest.
Arguments:
- tokens: bfloat16 [32, 512, 1024], P('dp', 'ctx'), may hold values from -6 to 6
- segments: int32 [32, 512], P('dp'), may hold values from 0 to 6, as said below
- query_weight: float32 [1024, 1024], P(('dp', 'ctx'), 'tp'), may hold values from -0.1875 to 0.1875
- key_weight: float32 [1024, 1024], P(('dp', 'ctx'), 'tp'), may hold values from -0.1875 to 0.1875
- value_weight: float32 [1024, 1024], P(('dp', 'ctx'), 'tp'), may hold values from -0.1875 to 0.1875
- out_weight: float32 [1024, 1024], P('tp', ('dp', 'ctx')), may hold values from -0.75 to 0.75
- up_weight: float32 [1024, 4096], P(('dp', 'ctx'), 'tp'), may hold values from -0.1875 to 0.1875
- down_weight: float32 [4096, 1024], P('tp', ('dp', 'ctx')), may hold values from -0.125 to 0.125
- query_bias: float32 [1024], P('tp'), may hold values from -3 to 3
- value_bias: float32 [1024], P('tp'), may hold values from -3 to 3
- out_bias: float32 [1024], replicated, may hold values from -3 to 3
- up_bias: float32 [4096], P('tp'), may hold values from -3 to 3
- down_bias: float32 [1024], replicated, may hold values from -3 to 3
- attn_gain: float32 [1024], replicated, may hold values from 0.5 to 1.5
- attn_shift: float32 [1024], replicated, may hold values from -3 to 3
- mlp_gain: float32 [1024], replicated, may hold values from 0.5 to 1.5
- mlp_shift: float32 [1024], replicated, may hold values from -3 to 3
- cotangent: bfloat16 [32, 512, 1024], P('dp', 'ctx'), may hold values from -6 to 6
Outputs:
- layer_out: bfloat16 [32, 512, 1024], P('dp', 'ctx')
- input_grad: bfloat16 [32, 512, 1024], P('dp', 'ctx')
- query_grad: float32 [1024, 1024], P(('dp', 'ctx'), 'tp')
- key_grad: float32 [1024, 1024], P(('dp', 'ctx'), 'tp')
- value_grad: float32 [1024, 1024], P(('dp', 'ctx'), 'tp')
- out_grad: float32 [1024, 1024], P('tp', ('dp', 'ctx'))
- up_grad: float32 [1024, 4096], P(('dp', 'ctx'), 'tp')
- down_grad: float32 [4096, 1024], P('tp', ('dp', 'ctx'))
- query_bias_grad: float32 [1024], P('tp')
- value_bias_grad: float32 [1024], P('tp')
- out_bias_grad: float32 [1024], replicated
- up_bias_grad: float32 [4096], P('tp')
- down_bias_grad: float32 [1024], replicated
- attn_gain_grad: float32 [1024], replicated
- attn_shift_grad: float32 [1024], replicated
- mlp_gain_grad: float32 [1024], replicated
- mlp_shift_grad: float32 [1024], replicated
Inputs may be any that keep to these rules, and one draw needn't show every extreme that they name: `segments`: segment numbers never fall along a sequence; every sequence holds a document that covers positions 128 to 384.
All inputs are finite; a program needn't handle non-finite values.
Results may differ from a plain program's by a relative error of at most 0.018.
Values may be sent and summed in bfloat16 or wider, within the bound.
No kernel may reach another device: no remote copies, remote signals or barrier semaphores. Data moves between devices by JAX's collectives and lax.ppermute only.
A program may use at most 192 MiB of HBM per device.

v0:
```python
import jax
import jax.numpy as jnp
from jax import lax
from jax.sharding import PartitionSpec as P

HEAD_DIM = 64


epsilon = 1e-12
root_half = 0.7071067811865476
inv_root_two_pi = 0.3989422804014327


def matmul(left, right):
    return jnp.dot(left, right, preferred_element_type=jnp.float32)


def rows_product(left, right):
    return lax.dot_general(
        left, right, (((0,), (0,)), ((), ())), preferred_element_type=jnp.float32
    )


def cols_product(left, right):
    return lax.dot_general(
        left, right, (((1,), (1,)), ((), ())), preferred_element_type=jnp.float32
    )


def norm_forward(values, gain, shift):
    centre = values - jnp.mean(values, axis=-1, keepdims=True)
    inverse = lax.rsqrt(jnp.mean(centre * centre, axis=-1, keepdims=True) + epsilon)
    normed = centre * inverse
    return (normed * gain + shift, normed, inverse)


def norm_backward(upstream, normed, inverse, gain):
    scaled = upstream * gain
    inner = scaled - jnp.mean(scaled, axis=-1, keepdims=True)
    inner = inner - normed * jnp.mean(scaled * normed, axis=-1, keepdims=True)
    return (inner * inverse, jnp.sum(upstream * normed, axis=0), jnp.sum(upstream, axis=0))


def masked_scores(query_heads, key_heads, allowed):
    factor = query_heads.shape[-1] ** (-0.5)
    scores = jnp.einsum(
        "sqhd,skhd->shqk", query_heads, key_heads, preferred_element_type=jnp.float32
    )
    return jnp.where(allowed, scores * factor, -1000000000.0)


def body(
    tokens,
    segments,
    query_weight,
    key_weight,
    value_weight,
    out_weight,
    up_weight,
    down_weight,
    query_bias,
    value_bias,
    out_bias,
    up_bias,
    down_bias,
    attn_gain,
    attn_shift,
    mlp_gain,
    mlp_shift,
    cotangent,
):
    seq_count, half_len, model_width = tokens.shape
    full_len = segments.shape[1]
    row_count = seq_count * half_len
    head_dim = HEAD_DIM
    heads_here = query_bias.shape[0] // head_dim
    factor = head_dim ** (-0.5)
    bf16 = jnp.bfloat16
    query_full, key_full, value_full, out_full = (
        lax.all_gather(query_weight.astype(bf16), ("dp", "ctx"), axis=0, tiled=True),
        lax.all_gather(key_weight.astype(bf16), ("dp", "ctx"), axis=0, tiled=True),
        lax.all_gather(value_weight.astype(bf16), ("dp", "ctx"), axis=0, tiled=True),
        lax.all_gather(out_weight.astype(bf16), ("dp", "ctx"), axis=1, tiled=True),
    )
    up_full, down_full = (
        lax.all_gather(up_weight.astype(bf16), ("dp", "ctx"), axis=0, tiled=True),
        lax.all_gather(down_weight.astype(bf16), ("dp", "ctx"), axis=1, tiled=True),
    )
    flat_input = tokens.reshape(row_count, model_width)
    queries = (matmul(flat_input, query_full) + query_bias).astype(bf16)
    keys_here = matmul(flat_input, key_full).astype(bf16)
    values_here = (matmul(flat_input, value_full) + value_bias).astype(bf16)
    key_all, value_all = (
        lax.all_gather(keys_here.reshape(seq_count, half_len, -1), "ctx", axis=1, tiled=True),
        lax.all_gather(values_here.reshape(seq_count, half_len, -1), "ctx", axis=1, tiled=True),
    )
    query_heads = queries.reshape(seq_count, half_len, heads_here, head_dim)
    key_heads = key_all.reshape(seq_count, full_len, heads_here, head_dim)
    value_heads = value_all.reshape(seq_count, full_len, heads_here, head_dim)
    local_segments = lax.dynamic_slice_in_dim(
        segments, lax.axis_index("ctx") * half_len, half_len, 1
    )
    allowed = local_segments[:, None, :, None] == segments[:, None, None, :]
    scores = masked_scores(query_heads, key_heads, allowed)
    largest = jnp.max(scores, axis=-1, keepdims=True)
    raised = jnp.exp(scores - largest)
    row_total = jnp.sum(raised, axis=-1, keepdims=True)
    attention = (raised / row_total).astype(bf16)
    log_total = largest + jnp.log(row_total)
    context = jnp.einsum(
        "shqk,skhd->sqhd", attention, value_heads, preferred_element_type=jnp.float32
    )
    context = context.reshape(row_count, -1).astype(bf16)
    attended = lax.psum(matmul(context, out_full), "tp")
    resid_one = flat_input.astype(jnp.float32) + attended + out_bias
    normed_one, unit_one, inverse_one = norm_forward(resid_one, attn_gain, attn_shift)
    normed_low = normed_one.astype(bf16)
    hidden_pre = matmul(normed_low, up_full) + up_bias
    erf_part = lax.erf(hidden_pre * root_half)
    hidden_act = (0.5 * hidden_pre * (1.0 + erf_part)).astype(bf16)
    mixed = lax.psum(matmul(hidden_act, down_full).astype(jnp.bfloat16), "tp").astype(jnp.float32)
    resid_two = normed_one + mixed + down_bias
    output, unit_two, inverse_two = norm_forward(resid_two, mlp_gain, mlp_shift)
    grad_output = cotangent.reshape(row_count, model_width).astype(jnp.float32)
    grad_two, mlp_gain_term, mlp_shift_term = norm_backward(
        grad_output, unit_two, inverse_two, mlp_gain
    )
    grad_mixed = grad_two.astype(bf16)
    down_bias_term = jnp.sum(grad_two, axis=0)
    down_term = rows_product(hidden_act, grad_mixed)
    grad_hidden = cols_product(grad_mixed, down_full)
    gelu_slope = (
        0.5 * (1.0 + erf_part)
        + hidden_pre * jnp.exp(-0.5 * hidden_pre * hidden_pre) * inv_root_two_pi
    )
    grad_pre = (grad_hidden * gelu_slope).astype(bf16)
    up_bias_term = jnp.sum(grad_pre.astype(jnp.float32), axis=0)
    up_term = rows_product(normed_low, grad_pre)
    grad_normed = grad_two + lax.psum(
        cols_product(grad_pre, up_full).astype(jnp.bfloat16), "tp"
    ).astype(jnp.float32)
    grad_one, attn_gain_term, attn_shift_term = norm_backward(
        grad_normed, unit_one, inverse_one, attn_gain
    )
    grad_attended = grad_one.astype(bf16)
    out_bias_term = jnp.sum(grad_one, axis=0)
    out_term = rows_product(context, grad_attended)
    grad_context = cols_product(grad_attended, out_full).astype(bf16)
    grad_context_heads = grad_context.reshape(seq_count, half_len, heads_here, head_dim)
    scores_again = masked_scores(query_heads, key_heads, allowed)
    probs_again = jnp.exp(scores_again - log_total)
    probs_low = probs_again.astype(bf16)
    grad_probs = jnp.einsum(
        "sqhd,skhd->shqk", grad_context_heads, value_heads, preferred_element_type=jnp.float32
    )
    row_inner = jnp.sum(probs_again * grad_probs, axis=-1, keepdims=True)
    grad_scores = (probs_again * (grad_probs - row_inner)).astype(bf16)
    grad_query = (
        jnp.einsum("shqk,skhd->sqhd", grad_scores, key_heads, preferred_element_type=jnp.float32)
        * factor
    )
    grad_key_all = (
        jnp.einsum("shqk,sqhd->skhd", grad_scores, query_heads, preferred_element_type=jnp.float32)
        * factor
    )
    grad_value_all = jnp.einsum(
        "shqk,sqhd->skhd", probs_low, grad_context_heads, preferred_element_type=jnp.float32
    )
    grad_key_here, grad_value_here = (
        lax.psum_scatter(
            grad_key_all.reshape(seq_count, full_len, -1).astype(jnp.bfloat16),
            "ctx",
            scatter_dimension=1,
            tiled=True,
        ).astype(jnp.float32),
        lax.psum_scatter(
            grad_value_all.reshape(seq_count, full_len, -1).astype(jnp.bfloat16),
            "ctx",
            scatter_dimension=1,
            tiled=True,
        ).astype(jnp.float32),
    )
    grad_query_low = grad_query.reshape(row_count, -1).astype(bf16)
    grad_key_low = grad_key_here.reshape(row_count, -1).astype(bf16)
    grad_value_low = grad_value_here.reshape(row_count, -1).astype(bf16)
    query_bias_term = jnp.sum(grad_query_low.astype(jnp.float32), axis=0)
    value_bias_term = jnp.sum(grad_value_low.astype(jnp.float32), axis=0)
    query_term = rows_product(flat_input, grad_query_low)
    key_term = rows_product(flat_input, grad_key_low)
    value_term = rows_product(flat_input, grad_value_low)
    sent_back = (
        cols_product(grad_query_low, query_full)
        + cols_product(grad_key_low, key_full)
        + cols_product(grad_value_low, value_full)
    )
    input_grad = grad_one + lax.psum(sent_back.astype(jnp.bfloat16), "tp").astype(jnp.float32)
    query_shard, key_shard, value_shard, out_shard, up_shard, down_shard = (
        lax.psum_scatter(query_term, ("dp", "ctx"), scatter_dimension=0, tiled=True),
        lax.psum_scatter(key_term, ("dp", "ctx"), scatter_dimension=0, tiled=True),
        lax.psum_scatter(value_term, ("dp", "ctx"), scatter_dimension=0, tiled=True),
        lax.psum_scatter(out_term, ("dp", "ctx"), scatter_dimension=1, tiled=True),
        lax.psum_scatter(up_term, ("dp", "ctx"), scatter_dimension=0, tiled=True),
        lax.psum_scatter(down_term, ("dp", "ctx"), scatter_dimension=1, tiled=True),
    )
    (
        query_bias_grad,
        value_bias_grad,
        up_bias_grad,
        out_bias_grad,
        down_bias_grad,
        attn_gain_grad,
        attn_shift_grad,
        mlp_gain_grad,
        mlp_shift_grad,
    ) = lax.psum(
        (
            query_bias_term,
            value_bias_term,
            up_bias_term,
            out_bias_term,
            down_bias_term,
            attn_gain_term,
            attn_shift_term,
            mlp_gain_term,
            mlp_shift_term,
        ),
        ("dp", "ctx"),
    )
    return (
        output.astype(bf16).reshape(seq_count, half_len, model_width),
        input_grad.astype(bf16).reshape(seq_count, half_len, model_width),
        query_shard,
        key_shard,
        value_shard,
        out_shard,
        up_shard,
        down_shard,
        query_bias_grad,
        value_bias_grad,
        out_bias_grad,
        up_bias_grad,
        down_bias_grad,
        attn_gain_grad,
        attn_shift_grad,
        mlp_gain_grad,
        mlp_shift_grad,
    )


def solution(mesh):
    placed = (
        P("dp", "ctx", None),
        P("dp", None),
        P(("dp", "ctx"), "tp"),
        P(("dp", "ctx"), "tp"),
        P(("dp", "ctx"), "tp"),
        P("tp", ("dp", "ctx")),
        P(("dp", "ctx"), "tp"),
        P("tp", ("dp", "ctx")),
        P("tp"),
        P("tp"),
        P(),
        P("tp"),
        P(),
        P(),
        P(),
        P(),
        P(),
        P("dp", "ctx", None),
    )
    return jax.shard_map(
        body,
        mesh=mesh,
        in_specs=placed,
        out_specs=(
            P("dp", "ctx", None),
            P("dp", "ctx", None),
            P(("dp", "ctx"), "tp"),
            P(("dp", "ctx"), "tp"),
            P(("dp", "ctx"), "tp"),
            P("tp", ("dp", "ctx")),
            P(("dp", "ctx"), "tp"),
            P("tp", ("dp", "ctx")),
            P("tp"),
            P("tp"),
            P(),
            P("tp"),
            P(),
            P(),
            P(),
            P(),
            P(),
        ),
        check_vma=False,
    )
```

profile of v0, /device:TPU:0, one launch (start us, length us, event | category | flops | bytes accessed | tf_op | source)
XLA Modules:
  0.0 1205.4 jit_solution(9934409496330059448)
XLA Ops:
  12.1 39.3 %all-gather.15.cloned.1.call-done = bf16[1024,512]{1,0:T(8,128)(2,1)} async-done(((bf16[64,512]{1,0:T(8,128)(2,1)}), bf16[1024,512]{1,0:T(8,128)(2,1)}) %all-gather.15.cloned.1.call-update) | async-done | bytes 1048592 | tf_op jit(solution)/shard_map/all_gather | solution.py:81
  55.8 35.3 %all-gather.9.cloned.1.call-done = bf16[1024,512]{1,0:T(8,128)(2,1)} async-done(((bf16[64,512]{1,0:T(8,128)(2,1)}), bf16[1024,512]{1,0:T(8,128)(2,1)}) %all-gather.9.cloned.1.call-update) | async-done | bytes 1048592 | tf_op jit(solution)/shard_map/all_gather | solution.py:82
  96.7 34.0 %all-gather.13.cloned.1.call-done = bf16[1024,512]{1,0:T(8,128)(2,1)} async-done(((bf16[64,512]{1,0:T(8,128)(2,1)}), bf16[1024,512]{1,0:T(8,128)(2,1)}) %all-gather.13.cloned.1.call-update) | async-done | bytes 1048592 | tf_op jit(solution)/shard_map/all_gather | solution.py:80
  135.4 6.7 all-gather.17.cloned.1.call-done
  149.9 6.6 copy-done
  163.1 8.6 fusion.24
  172.8 24.9 %all-gather.19.cloned.1.call-done = bf16[512,1024]{0,1:T(8,128)(2,1)} async-done(((bf16[512,64]{0,1:T(8,128)(2,1)}), bf16[512,1024]{0,1:T(8,128)(2,1)}) %all-gather.19.cloned.1.call-update) | async-done | bytes 1048592 | tf_op jit(solution)/shard_map/all_gather | solution.py:83
  205.1 104.1 %all-reduce.6.cloned.1.call-done = f32[1024,1024]{1,0:T(8,128)} async-done(((f32[1024,1024]{1,0:T(8,128)}), f32[1024,1024]{1,0:T(8,128)}) %all-reduce.6.cloned.1.call-update) | async-done | bytes 4194320 | tf_op jit(solution)/shard_map/psum | solution.py:114
  314.6 48.4 %all-gather.21.cloned.1.call-done = bf16[1024,2048]{1,0:T(8,128)(2,1)} async-done(((bf16[64,2048]{1,0:T(8,128)(2,1)}), bf16[1024,2048]{1,0:T(8,128)(2,1)}) %all-gather.21.cloned.1.call-update) | async-done | bytes 4194320 | tf_op jit(solution)/shard_map/all_gather | solution.py:86
  363.0 11.4 multiply_convert_fusion.1
  374.3 40.7 %all-gather.23.cloned.1.call-done = bf16[2048,1024]{0,1:T(8,128)(2,1)} async-done(((bf16[2048,64]{0,1:T(8,128)(2,1)}), bf16[2048,1024]{0,1:T(8,128)(2,1)}) %all-gather.23.cloned.1.call-update) | async-done | bytes 4194320 | tf_op jit(solution)/shard_map/all_gather | solution.py:87
  415.0 9.4 convolution_convert_fusion.1
  426.0 60.1 %all-reduce.8.cloned.1.call-done = bf16[1024,1024]{1,0:T(8,128)(2,1)} async-done(((bf16[1024,1024]{1,0:T(8,128)(2,1)}), bf16[1024,1024]{1,0:T(8,128)(2,1)}) %all-reduce.8.cloned.1.call-update) | async-done | bytes 2097168 | tf_op jit(solution)/shard_map/psum | solution.py:121
  497.1 7.6 convert_reduce_fusion
  506.7 5.7 convolution_convert_fusion
  512.7 62.8 %all-reduce.10.cloned.1.call-done = bf16[1024,1024]{1,0:T(8,128)(2,1)} async-done(((bf16[1024,1024]{1,0:T(8,128)(2,1)}), bf16[1024,1024]{1,0:T(8,128)(2,1)}) %all-reduce.10.cloned.1.call-update) | async-done | bytes 2097168 | tf_op jit(solution)/shard_map/psum | solution.py:139
  575.6 5.8 multiply_reduce_fusion.1
  592.0 11.8 multiply_reduce_fusion
  603.9 11.8 multiply_convert_fusion
  621.4 8.3 fusion.20
  634.3 6.1 convert_reduce_fusion.3
  650.3 6.5 add_convert_fusion.1
  656.9 5.0 fusion.26
  681.6 11.3 fusion.29
  693.1 12.3 %fusion.33 = f32[1024,2048]{1,0:T(8,128)} fusion(bf16[1024,2048]{1,0:T(8,128)(2,1)} %copy-done.41, f32[1024,1024]{1,0:T(8,128)} %copy-done.1, f32[1024]{0:T(1024)S(1)} %copy-done.32, f32[1024]{0:T(1024)S(1)} %copy-done.27, f32[1024]{0:T(1024)S(1)} %add_rsqrt_fusion.1, f32[1024]{0:T(1024)S(1)} %broadcast_multiply_fusion.4), kind=kOutput, calls=%fused_computation.83 | convolution fusion | flops 4300210176 | bytes 16793600 | tf_op jit(solution)/shard_map/dot_general | solution.py:19
  705.6 61.9 %all-reduce = (f32[512]{0:T(512)}, f32[512]{0:T(512)}, f32[1024]{0:T(1024)}, f32[2048]{0:T(1024)}, f32[1024]{0:T(1024)}, /*index=5*/f32[1024]{0:T(1024)}, f32[1024]{0:T(1024)}, f32[1024]{0:T(1024)}, f32[1024]{0:T(1024)}) all-reduce(f32[512]{0:T(512)S(1)} %reduce_sum.184, ...), channel_id=1, replica_groups=mesh['dp'=8,'ctx'=2,'tp'=2] {'dp','ctx'}, use_global_device_ids=true, to_apply=%region_24.25 | all-reduce | flops 9216 | bytes 73728 | tf_op jit(solution)/shard_map/psum | solution.py:215
  772.5 13.3 %reduce-scatter.19.cloned.1.call-done = f32[512,64]{0,1:T(8,128)} async-done(((f32[512,1024]{0,1:T(8,128)}), f32[512,64]{0,1:T(8,128)}) %reduce-scatter.19.cloned.1.call-update) | async-done | bytes 131088 | tf_op jit(solution)/shard_map/reduce_scatter | solution.py:201
  785.9 65.3 %reduce-scatter.25.cloned.1.call-done = f32[64,512]{1,0:T(8,128)} async-done(((f32[1024,512]{1,0:T(8,128)}), f32[64,512]{1,0:T(8,128)}) %reduce-scatter.25.cloned.1.call-update) | async-done | bytes 131088
  851.2 64.7 %reduce-scatter.29.cloned.1.call-done = f32[64,512]{1,0:T(8,128)} async-done(((f32[1024,512]{1,0:T(8,128)}), f32[64,512]{1,0:T(8,128)}) %reduce-scatter.29.cloned.1.call-update) | async-done | bytes 131088
  915.9 65.2 %reduce-scatter.27.cloned.1.call-done = f32[64,512]{1,0:T(8,128)} async-done(((f32[1024,512]{1,0:T(8,128)}), f32[64,512]{1,0:T(8,128)}) %reduce-scatter.27.cloned.1.call-update) | async-done | bytes 131088
  981.0 108.3 %reduce-scatter.23.cloned.1.call-done = f32[2048,64]{0,1:T(8,128)} async-done(((f32[2048,1024]{0,1:T(8,128)}), f32[2048,64]{0,1:T(8,128)}) %reduce-scatter.23.cloned.1.call-update) | async-done | bytes 524304 | tf_op jit(solution)/shard_map/reduce_scatter | solution.py:203
  1089.3 109.0 %reduce-scatter.21.cloned.1.call-done = f32[64,2048]{1,0:T(8,128)} async-done(((f32[1024,2048]{1,0:T(8,128)}), f32[64,2048]{1,0:T(8,128)}) %reduce-scatter.21.cloned.1.call-update) | async-done | bytes 524304 | tf_op jit(solution)/shard_map/reduce_scatter | solution.py:202
  (188 shorter events, 118.0 us)
Async XLA Ops:
  7.2 44.2 %all-gather.15.cloned.1.call-start = ((), (), s32[]{:S(2)}) async-start(), calls=%async_computation.11 | async-start | bytes 1114112 | tf_op jit(solution)/shard_map/all_gather | solution.py:81
  8.8 82.2 %all-gather.9.cloned.1.call-start = ((), (), s32[]{:S(2)}) async-start(), calls=%async_computation.8 | async-start | bytes 1114112 | tf_op jit(solution)/shard_map/all_gather | solution.py:82
  10.4 120.3 %all-gather.13.cloned.1.call-start = ((), (), s32[]{:S(2)}) async-start(), calls=%async_computation.10 | async-start | bytes 1114112 | tf_op jit(solution)/shard_map/all_gather | solution.py:80
  12.0 130.1 %all-gather.17.cloned.1.call-start = ((), (), s32[]{:S(2)}) async-start(), calls=%async_computation.12 | async-start | bytes 3145728 | tf_op jit(solution)/shard_map/all_gather | solution.py:94
  51.4 39.6 %copy-start.9 = (bf16[4,256,1024]{2,1,0:T(8,128)(2,1)S(1)}, bf16[4,256,1024]{2,1,0:T(8,128)(2,1)}, u32[]{:S(2)}) copy-start(bf16[4,256,1024]{2,1,0:T(8,128)(2,1)} %param.18) | copy-start | bytes 6291460
  51.4 39.6 %copy-start.39 = (f32[512]{0:T(512)S(1)}, f32[512]{0:T(512)}, u32[]{:S(2)}) copy-start(f32[512]{0:T(512)} %param.27) | copy-start | bytes 6148
  55.7 38.9 %copy-start.25 = (f32[512,64]{0,1:T(8,128)S(1)}, f32[512,64]{0,1:T(8,128)}, u32[]{:S(2)}) copy-start(f32[512,64]{0,1:T(8,128)} %param.23) | copy-start | bytes 393220
  55.7 39.8 %copy-start.28 = (s32[4,512]{1,0:T(4,128)S(1)}, s32[4,512]{1,0:T(4,128)}, u32[]{:S(2)}) copy-start(s32[4,512]{1,0:T(4,128)} %param.19) | copy-start | bytes 24580
  55.7 75.0 %copy-start.40 = (f32[512]{0:T(512)S(1)}, f32[512]{0:T(512)}, u32[]{:S(2)}) copy-start(f32[512]{0:T(512)} %param.26) | copy-start | bytes 6148
  55.7 104.6 %all-gather.11.cloned.1.call-start = ((), (), s32[]{:S(2)}) async-start(), calls=%async_computation.9 | async-start | bytes 3145728 | tf_op jit(solution)/shard_map/all_gather | solution.py:95
  94.5 103.2 %all-gather.19.cloned.1.call-start = ((), (), s32[]{:S(2)}) async-start(), calls=%async_computation.13 | async-start | bytes 1114112 | tf_op jit(solution)/shard_map/all_gather | solution.py:83
  95.2 214.0 %all-reduce.6.cloned.1.call-start = ((), (), s32[]{:S(2)}) async-start(), calls=%async_computation.14 | async-start | bytes 8388608 | tf_op jit(solution)/shard_map/psum | solution.py:114
  172.8 24.9 %copy-start.19 = (bf16[64,8,4,256]{3,1,2,0:T(8,128)(2,1)}, bf16[64,8,4,256]{3,1,2,0:T(8,128)(2,1)S(1)}, u32[]{:S(2)}) copy-start(bf16[64,8,4,256]{3,1,2,0:T(8,128)(2,1)S(1)} %copy.90) | copy-start | bytes 3145732
  202.3 107.0 %copy-start.10 = (bf16[4,256,1024]{2,1,0:T(8,128)(2,1)S(1)}, bf16[4,256,1024]{2,1,0:T(8,128)(2,1)}, u32[]{:S(2)}) copy-start(bf16[4,256,1024]{2,1,0:T(8,128)(2,1)} %param.18) | copy-start | bytes 6291460
  202.3 107.0 %copy-start.29 = (f32[1024]{0:T(1024)S(1)}, f32[1024]{0:T(1024)}, u32[]{:S(2)}) copy-start(f32[1024]{0:T(1024)} %param.28) | copy-start | bytes 12292
  202.3 160.7 %all-gather.21.cloned.1.call-start = ((), (), s32[]{:S(2)}) async-start(), calls=%async_computation.15 | async-start | bytes 4456448 | tf_op jit(solution)/shard_map/all_gather | solution.py:86
  204.0 211.0 %all-gather.23.cloned.1.call-start = ((), (), s32[]{:S(2)}) async-start(), calls=%async_computation.16 | async-start | bytes 4456448 | tf_op jit(solution)/shard_map/all_gather | solution.py:87
  204.9 281.2 %all-reduce.8.cloned.1.call-start = ((), (), s32[]{:S(2)}) async-start(), calls=%async_computation.17 | async-start | bytes 4194304 | tf_op jit(solution)/shard_map/psum | solution.py:121
  312.0 50.9 %copy-start.27 = (f32[1024]{0:T(1024)S(1)}, f32[1024]{0:T(1024)}, u32[]{:S(2)}) copy-start(f32[1024]{0:T(1024)} %param.31) | copy-start | bytes 12292
  312.1 50.9 %copy-start.32 = (f32[1024]{0:T(1024)S(1)}, f32[1024]{0:T(1024)}, u32[]{:S(2)}) copy-start(f32[1024]{0:T(1024)} %param.32) | copy-start | bytes 12292
  312.1 50.9 %copy-start.38 = (f32[2048]{0:T(1024)S(1)}, f32[2048]{0:T(1024)}, u32[]{:S(2)}) copy-start(f32[2048]{0:T(1024)} %param.29) | copy-start | bytes 24580
  424.5 61.6 %copy-start.30 = (f32[1024]{0:T(1024)S(1)}, f32[1024]{0:T(1024)}, u32[]{:S(2)}) copy-start(f32[1024]{0:T(1024)} %param.30) | copy-start | bytes 12292
  424.5 151.1 %all-reduce.10.cloned.1.call-start = ((), (), s32[]{:S(2)}) async-start(), calls=%async_computation.18 | async-start | bytes 4194304 | tf_op jit(solution)/shard_map/psum | solution.py:139
  512.5 133.3 %reduce-scatter.15.cloned.1.call-start = ((), (), s32[]{:S(2)}) async-start(), calls=%async_computation.19 | async-start | bytes 3145728 | tf_op jit(solution)/shard_map/reduce_scatter | solution.py:170
  621.4 28.9 %reduce-scatter.17.cloned.1.call-start = ((), (), s32[]{:S(2)}) async-start(), calls=%async_computation.20 | async-start | bytes 3145728 | tf_op jit(solution)/shard_map/reduce_scatter | solution.py:176
  634.1 133.5 %all-reduce.12.cloned.1.call-start = ((), (), s32[]{:S(2)}) async-start(), calls=%async_computation.21 | async-start | bytes 4194304 | tf_op jit(solution)/shard_map/psum | solution.py:196
  656.8 129.1 %reduce-scatter.19.cloned.1.call-start = ((), (), s32[]{:S(2)}) async-start(), calls=%async_computation.22 | async-start | bytes 2228224 | tf_op jit(solution)/shard_map/reduce_scatter | solution.py:201
  661.9 189.3 %reduce-scatter.25.cloned.1.call-start = ((), (), s32[]{:S(2)}) async-start(), calls=%async_computation.25 | async-start | bytes 2228224
  669.0 246.9 %reduce-scatter.29.cloned.1.call-start = ((), (), s32[]{:S(2)}) async-start(), calls=%async_computation.27 | async-start | bytes 2228224
  674.6 306.5 %reduce-scatter.27.cloned.1.call-start = ((), (), s32[]{:S(2)}) async-start(), calls=%async_computation.26 | async-start | bytes 2228224
  681.3 408.0 %reduce-scatter.23.cloned.1.call-start = ((), (), s32[]{:S(2)}) async-start(), calls=%async_computation.24 | async-start | bytes 8912896 | tf_op jit(solution)/shard_map/reduce_scatter | solution.py:203
  693.0 505.3 %reduce-scatter.21.cloned.1.call-start = ((), (), s32[]{:S(2)}) async-start(), calls=%async_computation.23 | async-start | bytes 8912896 | tf_op jit(solution)/shard_map/reduce_scatter | solution.py:202
  (32 other events, 170.6 us)
Sparse Core Ops, SparseCore 0:
  10.8 40.6 all-gather.14
  54.2 36.8 all-gather.8
  93.8 36.8 all-gather.12
  132.7 9.4 all-gather.16
  144.1 11.7 all-gather.10
  158.5 39.1 all-gather.18
  202.4 106.7 all-reduce.5
  312.2 50.7 all-gather.20
  365.9 49.0 all-gather.22
  424.6 61.3 all-reduce.7
  512.6 62.9 all-reduce.9
  621.5 9.6 reduce-scatter.14
  634.2 9.9 reduce-scatter.16
  656.9 62.8 all-reduce.11
  724.0 61.8 reduce-scatter.18
  790.5 60.6 reduce-scatter.24
  855.3 60.5 reduce-scatter.28
  920.5 60.4 reduce-scatter.26
  985.7 103.6 reduce-scatter.22
  1093.8 104.4 reduce-scatter.20
where the time goes:
time: 1210 us
  waiting for transfers between devices  882 us (73%)
  matrix products  145 us (12%)
  blocking collectives  61.9 us (5%)
  other arithmetic  49.9 us (4%)
  local copies, waits for them, and re-layouts  49.1 us (4%)
  between operations  15.2 us (1%)
    unnamed x23, waiting for transfers between devices  195 us
    reduce_scatter x1, waiting for transfers between devices, body(): lax.psum_scatter(up_term, ('dp', 'ctx'), scatter_dimension=0, tiled=True)  109 us
    reduce_scatter x1, waiting for transfers between devices, body(): lax.psum_scatter(down_term, ('dp', 'ctx'), scatter_dimension=1, tiled=True)  108 us
    psum x1, waiting for transfers between devices, body(): attended = lax.psum(matmul(context, out_full), 'tp')  104 us
    psum x1, waiting for transfers between devices, body(): lax.psum(cols_product(grad_pre, up_full).astype(jnp.bfloat16), 'tp')  62.8 us
    psum x1, blocking collectives, body(): lax.psum((query_bias_term, value_bias_term, up_bias_term, out_bias_term,...  61.9 us
    psum x1, waiting for transfers between devices, body(): lax.psum(matmul(hidden_act, down_full).astype(jnp.bfloat16), 'tp')  60.1 us
    all_gather x1, waiting for transfers between devices, body(): lax.all_gather(up_weight.astype(bf16), ('dp', 'ctx'), axis=0, tiled=True)  48.4 us
  transfers between devices with their start and end apart: 20, of which 16 were waited for; matrix products, arithmetic and copies ran while one was open for 12% of the time, Pallas kernels for 0%

commit v1 on v0

v1 whole, which is shorter than its diff:
```python
import jax
import jax.numpy as jnp
from jax import lax
from jax.sharding import PartitionSpec as P

HEAD_DIM = 64

epsilon = 1e-12
root_half = 0.7071067811865476
inv_root_two_pi = 0.3989422804014327
bf16 = jnp.bfloat16
f32 = jnp.float32


def matmul(left, right):
    return jnp.dot(left, right, preferred_element_type=f32)


def rows_product(left, right):
    return lax.dot_general(left, right, (((0,), (0,)), ((), ())), preferred_element_type=f32)


def cols_product(left, right):
    return lax.dot_general(left, right, (((1,), (1,)), ((), ())), preferred_element_type=f32)


def norm_forward(values, gain, shift):
    centre = values - jnp.mean(values, axis=-1, keepdims=True)
    inverse = lax.rsqrt(jnp.mean(centre * centre, axis=-1, keepdims=True) + epsilon)
    normed = centre * inverse
    return (normed * gain + shift, normed, inverse)


def norm_backward(upstream, normed, inverse, gain):
    scaled = upstream * gain
    inner = scaled - jnp.mean(scaled, axis=-1, keepdims=True)
    inner = inner - normed * jnp.mean(scaled * normed, axis=-1, keepdims=True)
    return (inner * inverse, jnp.sum(upstream * normed, axis=0), jnp.sum(upstream, axis=0))


def swap(values, axis):
    return lax.ppermute(values, axis, [(0, 1), (1, 0)])


def take(values, index, axis):
    return lax.dynamic_index_in_dim(values, index, axis, keepdims=False)


def add(left, right):
    return (left.astype(f32) + right.astype(f32)).astype(bf16)


def gather_all(shard):
    full = lax.all_gather(shard, ("tp", "dp", "ctx"), axis=0, tiled=True)
    return full.reshape(2, -1, shard.shape[-1])


def scatter_sum(grad, dp_count):
    rows, _, cols = grad.shape
    t = lax.axis_index("tp")
    if dp_count != 8:
        mine = lax.psum_scatter(grad, "tp", scatter_dimension=1, tiled=True)
        mine = mine.reshape(rows, cols)
        return lax.psum_scatter(mine, "dp", scatter_dimension=0, tiled=True).astype(f32)
    d = lax.axis_index("dp")
    x, z = d % 2, d // 2
    piece = rows // 8
    blocks = grad.reshape(2, 2, 2, piece, 2, cols)
    over_x = [(i, i ^ 1) for i in range(8)]
    first, second = blocks[0], blocks[1]
    got = swap(take(first, 1 - t, 3), "tp")
    got_b = lax.ppermute(take(second, 1 - x, 1), "dp", over_x)
    first = add(take(first, t, 3), got)
    second = add(take(second, x, 1), got_b)
    got = lax.ppermute(take(first, 1 - x, 1), "dp", over_x)
    got_b = swap(take(second, 1 - t, 2), "tp")
    first = add(take(first, x, 1), got)
    second = add(take(second, t, 2), got_b)
    line = jnp.concatenate([first, second], axis=0)
    total = take(line, z, 0).astype(f32)
    for step in range(1, 4):
        pairs = [(i, (i + 2 * step) % 8) for i in range(8)]
        got = lax.ppermute(take(line, (z + step) % 4, 0), "dp", pairs)
        total = total + got.astype(f32)
    return total


def to_shard(total, c):
    halves = total.reshape(2, total.shape[0] // 2, total.shape[1])
    mine = take(halves, c, 0)
    other = swap(take(halves, 1 - c, 0), "ctx")
    ordered = jnp.where(c == 0, jnp.stack([mine, other], 1), jnp.stack([other, mine], 1))
    return ordered


def body(dp_count, tokens, segments, query_weight, key_weight, value_weight, out_weight, up_weight, down_weight, query_bias, value_bias, out_bias, up_bias, down_bias, attn_gain, attn_shift, mlp_gain, mlp_shift, cotangent):
    c = lax.axis_index("ctx")
    t = lax.axis_index("tp")
    half, width = tokens.shape[1], tokens.shape[2]
    rows = 2 * half
    factor = HEAD_DIM ** (-0.5)
    heads = 2 * query_bias.shape[0] // HEAD_DIM
    ff = 2 * up_bias.shape[0]
    inner = heads * HEAD_DIM

    shard_one = jnp.concatenate([query_weight, key_weight, value_weight, out_weight.T], 1).astype(bf16)
    full_one = gather_all(shard_one)
    full_up = gather_all(up_weight.astype(bf16))
    full_down = gather_all(down_weight.T.astype(bf16))
    hin = inner // 2

    seq = 2 * t + c
    other_seq = 2 * t + 1 - c
    mine_pair = jnp.stack([take(tokens, seq, 0), take(cotangent, seq, 0)])
    send_pair = jnp.stack([take(tokens, other_seq, 0), take(cotangent, other_seq, 0)])
    got_pair = swap(send_pair, "ctx")
    flat = jnp.concatenate([mine_pair[0], got_pair[0]], 0)
    grad_output = jnp.concatenate([mine_pair[1], got_pair[1]], 0).astype(f32)
    seg = take(segments, seq, 0)
    seg = jnp.where(c == 0, seg, jnp.roll(seg, half))
    allowed = seg[:, None] == seg[None, :]

    bias_q = lax.all_gather(query_bias, "tp", axis=0, tiled=True)
    bias_v = lax.all_gather(value_bias, "tp", axis=0, tiled=True)
    bias_up = lax.all_gather(up_bias, "tp", axis=0, tiled=True)

    def whole(part):
        return jnp.concatenate([part[0], part[1]], axis=1)

    w_q = whole(full_one[:, :, :hin])
    w_k = whole(full_one[:, :, hin : 2 * hin])
    w_v = whole(full_one[:, :, 2 * hin : 3 * hin])
    w_ot = whole(full_one[:, :, 3 * hin :])
    w_up = whole(full_up)
    w_dt = whole(full_down)

    queries = (matmul(flat, w_q) + bias_q).astype(bf16)
    keys = matmul(flat, w_k).astype(bf16)
    values = (matmul(flat, w_v) + bias_v).astype(bf16)
    qh = queries.reshape(rows, heads, HEAD_DIM)
    kh = keys.reshape(rows, heads, HEAD_DIM)
    vh = values.reshape(rows, heads, HEAD_DIM)
    scores = jnp.einsum("qhd,khd->hqk", qh, kh, preferred_element_type=f32)
    scores = jnp.where(allowed, scores * factor, -1000000000.0)
    raised = jnp.exp(scores - jnp.max(scores, axis=-1, keepdims=True))
    probs = (raised / jnp.sum(raised, axis=-1, keepdims=True)).astype(bf16)
    context = jnp.einsum("hqk,khd->qhd", probs, vh, preferred_element_type=f32)
    context = context.reshape(rows, -1).astype(bf16)
    resid_one = flat.astype(f32) + cols_product(context, w_ot) + out_bias
    normed_one, unit_one, inverse_one = norm_forward(resid_one, attn_gain, attn_shift)
    normed_low = normed_one.astype(bf16)
    hidden_pre = matmul(normed_low, w_up) + bias_up
    erf_part = lax.erf(hidden_pre * root_half)
    hidden_act = (0.5 * hidden_pre * (1.0 + erf_part)).astype(bf16)
    slope = (0.5 * (1.0 + erf_part) + hidden_pre * jnp.exp(-0.5 * hidden_pre * hidden_pre) * inv_root_two_pi)
    resid_two = normed_one + cols_product(hidden_act, w_dt) + down_bias
    output, unit_two, inverse_two = norm_forward(resid_two, mlp_gain, mlp_shift)
    grad_two, mlp_gain_term, mlp_shift_term = norm_backward(grad_output, unit_two, inverse_two, mlp_gain)
    grad_mixed = grad_two.astype(bf16)
    down_bias_term = jnp.sum(grad_two, axis=0)
    grad_pre = (matmul(grad_mixed, w_dt) * slope).astype(bf16)
    up_bias_term = jnp.sum(grad_pre.astype(f32), axis=0)

    def both(values):
        return jnp.concatenate([values, swap(values, "ctx")], 0)

    def halves(values):
        parts = values.reshape(rows, 2, 2, -1)
        return jnp.concatenate([take(parts, c, 2), swap(take(parts, 1 - c, 2), "ctx")], 0)

    def grads(left, right):
        out = rows_product(left, right.reshape(2 * rows, -1)).astype(bf16)
        return out.reshape(width, 2, -1)

    down_total = scatter_sum(grads(both(grad_mixed), halves(hidden_act)), dp_count)
    up_total = scatter_sum(grads(both(normed_low), halves(grad_pre)), dp_count)

    grad_normed = grad_two + cols_product(grad_pre, w_up)
    grad_one, attn_gain_term, attn_shift_term = norm_backward(grad_normed, unit_one, inverse_one, attn_gain)
    grad_attended = grad_one.astype(bf16)
    out_bias_term = jnp.sum(grad_one, axis=0)
    grad_context = matmul(grad_attended, w_ot).astype(bf16).reshape(rows, heads, HEAD_DIM)
    grad_probs = jnp.einsum("qhd,khd->hqk", grad_context, vh, preferred_element_type=f32)
    probs_wide = probs.astype(f32)
    row_inner = jnp.sum(probs_wide * grad_probs, axis=-1, keepdims=True)
    grad_scores = (probs_wide * (grad_probs - row_inner)).astype(bf16)
    grad_q = jnp.einsum("hqk,khd->qhd", grad_scores, kh, preferred_element_type=f32) * factor
    grad_k = jnp.einsum("hqk,qhd->khd", grad_scores, qh, preferred_element_type=f32) * factor
    grad_v = jnp.einsum("hqk,qhd->khd", probs, grad_context, preferred_element_type=f32)
    grad_q = grad_q.reshape(rows, -1).astype(bf16)
    grad_k = grad_k.reshape(rows, -1).astype(bf16)
    grad_v = grad_v.reshape(rows, -1).astype(bf16)
    query_bias_term = jnp.sum(grad_q.astype(f32), axis=0)
    value_bias_term = jnp.sum(grad_v.astype(f32), axis=0)
    sent_back = cols_product(grad_q, w_q) + cols_product(grad_k, w_k) + cols_product(grad_v, w_v)
    input_grad = (grad_one + sent_back).astype(bf16)

    both_x = both(flat)
    one_grad = jnp.concatenate(
        [grads(both_x, halves(grad_q)), grads(both_x, halves(grad_k)), grads(both_x, halves(grad_v)), grads(both(grad_attended), halves(context))],
        axis=2,
    )
    one_total = scatter_sum(one_grad, dp_count)

    small = jnp.concatenate(
        [query_bias_term, value_bias_term, up_bias_term, out_bias_term, down_bias_term, attn_gain_term, attn_shift_term, mlp_gain_term, mlp_shift_term]
    )
    small = lax.psum(small.reshape(-1, 128), ("dp", "ctx", "tp")).reshape(-1)

    def cut(start, size):
        return lax.slice_in_dim(small, start, start + size)

    def cut_tp(start, size):
        return lax.dynamic_slice_in_dim(small, start + t * (size // 2), size // 2)

    at = 2 * inner + ff
    vectors = [cut(at + i * width, width) for i in range(6)]

    def spread(values):
        mine, theirs = values[:half], values[half:]
        got = swap(theirs, "ctx")
        pair = jnp.where(c == 0, jnp.stack([mine, got]), jnp.stack([got, mine]))
        far = swap(pair, "tp")
        return jnp.where(t == 0, jnp.concatenate([pair, far]), jnp.concatenate([far, pair]))

    one_shard = to_shard(one_total, c)
    r = one_shard.shape[0]
    one_shard = one_shard.reshape(r, 2, 4, -1).transpose(2, 0, 1, 3).reshape(4, r, -1)
    up_shard = to_shard(up_total, c).reshape(r, -1)
    down_shard = to_shard(down_total, c).reshape(r, -1).T
    return (
        spread(output.astype(bf16)),
        spread(input_grad),
        one_shard[0],
        one_shard[1],
        one_shard[2],
        one_shard[3].T,
        up_shard,
        down_shard,
        cut_tp(0, inner),
        cut_tp(inner, inner),
        vectors[0],
        cut_tp(2 * inner, ff),
        *vectors[1:],
    )


def solution(mesh):
    weight_in, weight_out = P(("dp", "ctx"), "tp"), P("tp", ("dp", "ctx"))
    rows = P("dp", "ctx", None)
    weights = (weight_in, weight_in, weight_in, weight_out, weight_in, weight_out)
    vectors = (P("tp"), P("tp"), P(), P("tp"), P(), P(), P(), P(), P())
    dp_count = mesh.shape["dp"]

    def run(*args):
        return body(dp_count, *args)

    return jax.shard_map(
        run,
        mesh=mesh,
        in_specs=(rows, P("dp", None), *weights, *vectors, rows),
        out_specs=(rows, rows, *weights, *vectors),
        check_vma=False,
    )
```

time: 1210 us -> 724 us (0.60)
  waiting for transfers between devices: 882 us -> 236 us
  local copies, waits for them, and re-layouts: 49.1 us -> 183 us
  starting transfers between devices: 2.26 us -> 37 us
  matrix products: 145 us -> 115 us
  other arithmetic: 49.9 us -> 71.1 us
    reduce_scatter x5 -> x0, waiting for transfers between devices: 231 us -> none  [the longest x1 109 us: body(): lax.psum_scatter(up_term, ('dp', 'ctx'), scatter_dimension=0, tiled=True)]
    psum x4 -> x0, waiting for transfers between devices: 227 us -> none  [the longest x1 104 us: body(): attended = lax.psum(matmul(context, out_full), 'tp')]
    unnamed x23 -> x3, waiting for transfers between devices: 195 us -> 0.05 us
    ppermute x0 -> x39, waiting for transfers between devices: none -> 81.8 us  [the longest x24 43.9 us: swap(): return lax.ppermute(values, axis, [(0, 1), (1, 0)])]
    all_gather x8 -> x3, waiting for transfers between devices: 229 us -> 154 us  [gather_all(): full = lax.all_gather(shard, ('tp', 'dp', 'ctx'), axis=0, tiled=True)]
    dynamic_slice x1 -> x19, local copies, waits for them, and re-layouts: 0.01 us -> 47.6 us  [the longest x17 46.3 us: take(): return lax.dynamic_index_in_dim(values, index, axis, keepdims=False)]
    ppermute x0 -> x39, starting transfers between devices: none -> 36.9 us  [the longest x9 17 us: scatter_sum(): got = lax.ppermute(take(line, (z + step) % 4, 0), 'dp', pairs)]
    squeeze x0 -> x16, local copies, waits for them, and re-layouts: none -> 29 us  [the longest x4 13.6 us: scatter_sum(): first, second = (blocks[0], blocks[1])]
  transfers between devices with their start and end apart: 20 -> 42, of which waited for: 16 -> 14; matrix products, arithmetic and copies ran while one was open for 12% -> 49% of each run, Pallas kernels for 0% -> 0%
where the time goes in v1:
time: 724 us; the launch traced here: 711 us
  waiting for transfers between devices  236 us (33%)
  local copies, waits for them, and re-layouts  183 us (25%)
  matrix products  115 us (16%)
  other arithmetic  71.1 us (10%)
  blocking collectives  53.7 us (7%)
  starting transfers between devices  37 us (5%)
  between operations  15.5 us (2%)
    all_gather x3, waiting for transfers between devices, gather_all(): full = lax.all_gather(shard, ('tp', 'dp', 'ctx'), axis=0, tiled=True)  154 us
    unnamed x168, local copies, waits for them, and re-layouts  46.4 us
    dynamic_slice x17, local copies, waits for them, and re-layouts, take(): return lax.dynamic_index_in_dim(values, index, axis, keepdims=False)  46.3 us
    ppermute x24, waiting for transfers between devices, swap(): return lax.ppermute(values, axis, [(0, 1), (1, 0)])  43.9 us
    psum x1, blocking collectives, body(): small = lax.psum(small.reshape(-1, 128), ('dp', 'ctx', 'tp')).reshape(-1)  39.8 us
    dot_general x6, matrix products, matmul(): return jnp.dot(left, right, preferred_element_type=f32)  34.7 us
    ppermute x9, waiting for transfers between devices, scatter_sum(): got = lax.ppermute(take(line, (z + step) % 4, 0), 'dp', pairs)  31.7 us
    dot_general x6, matrix products, rows_product(): lax.dot_general(left, right, (((0,), (0,)), ((), ())), preferred_element_...  28.7 us
  transfers between devices with their start and end apart: 42, of which 14 were waited for; matrix products, arithmetic and copies ran while one was open for 49% of the time, Pallas kernels for 0%

profile of v1, /device:TPU:0, one launch (start us, length us, event | category | flops | bytes accessed | tf_op | source)
XLA Modules:
  0.0 710.8 jit_solution(13122932312731177195)
XLA Ops:
  17.1 5.2 all-gather.1
  33.3 58.9 %all-gather.6.cloned.1.call-done = bf16[2048,2048]{1,0:T(8,128)(2,1)} async-done(((bf16[64,2048]{1,0:T(8,128)(2,1)}), bf16[2048,2048]{1,0:T(8,128)(2,1)}) %all-gather.6.cloned.1.call-update) | async-done | bytes 8388624 | tf_op jit(solution)/shard_map/all_gather | solution.py:54
  92.2 5.7 slice_bitcast_fusion.1
  114.7 9.6 %fusion.143 = (f32[16,512]{1,0:T(8,128)S(1)}, f32[16,512,512]{1,2,0:T(8,128)}) fusion(pred[512,512]{0,1:T(8,128)(4,1)S(1)} %broadcast_compare_fusion, bf16[512,16,64]{0,2,1:T(8,128)(2,1)S(1)} %bitcast.291, bf16[512,16,64]{0,2,1:T(8,128)(2,1)S(1)} %bitcast.287), kind=kOutput, calls=%fused_computation.321 | convolution fusion | flops 553648640 | bytes 19169280 | tf_op jit(solution)/shard_map/sub | solution.py:145
  124.4 6.8 divide_convert_fusion
  138.9 32.2 %all-gather.8.cloned.1.call-done = bf16[2048,2048]{1,0:T(8,128)(2,1)} async-done(((bf16[64,2048]{1,0:T(8,128)(2,1)}), bf16[2048,2048]{1,0:T(8,128)(2,1)}) %all-gather.8.cloned.1.call-update) | async-done | bytes 8388624 | tf_op jit(solution)/shard_map/all_gather | solution.py:54
  178.1 9.3 %multiply_convert_fusion = (bf16[512,4096]{1,0:T(8,128)(2,1)}, f32[512,4096]{1,0:T(8,128)}) fusion(f32[4096]{0:T(1024)S(1)} %all_gather.22, bf16[512,1024]{1,0:T(8,128)(2,1)} %fusion.53, bf16[1024,2048]{1,0:T(8,128)(2,1)S(1)} %get-tuple-element.34, bf16[1024,2048]{1,0:T(8,128)(2,1)S(1)} %get-tuple-element.33), kind=kOutput, calls=%fused_computation.19 | convolution fusion | flops 4324327424 | bytes 22036480 | tf_op jit(solution)/shard_map/dot_general | solution.py:16
  187.5 62.6 %all-gather.10.cloned.1.call-done = bf16[2048,2048]{1,0:T(8,128)(2,1)} async-done(((bf16[64,2048]{1,0:T(8,128)(2,1)}), bf16[2048,2048]{1,0:T(8,128)(2,1)}) %all-gather.10.cloned.1.call-update) | async-done | bytes 8388624 | tf_op jit(solution)/shard_map/all_gather | solution.py:54
  254.7 4.8 fusion.145
  265.1 11.8 %convert_reduce_fusion = (f32[4096]{0:T(1024)S(1)}, bf16[512,4096]{1,0:T(8,128)(2,1)S(1)}) fusion(f32[512,4096]{1,0:T(8,128)} %get-tuple-element.114, f32[4096]{0:T(1024)S(1)} %all_gather.22, bf16[512,1024]{1,0:T(8,128)(2,1)} %convert_element_type.353, bf16[1024,2048]{1,0:T(8,128)(2,1)} %copy-done.36, bf16[1024,2048]{1,0:T(8,128)(2,1)} %copy-done.35), kind=kOutput, calls=%fused_computation.18 | convolution fusion | flops 4339003392 | bytes 22052864 | tf_op jit(solution)/shard_map/dot_general | solution.py:16
  276.9 9.0 %multiply_reduce_fusion = (f32[1024]{0:T(1024)S(1)}, f32[512]{0:T(512)S(1)}, f32[512]{0:T(512)S(1)}, f32[1024]{0:T(1024)S(1)}, f32[512,1024]{1,0:T(8,128)S(1)}) fusion(f32[512,1024]{1,0:T(8,128)S(1)} %get-tuple-element.112, f32[512]{0:T(512)S(1)} %add_rsqrt_fusion.1, f32[512]{0:T(512)S(1)} %broadcast_multiply_fusion.5, f32[1024]{0:T(1024)S(1)} %copy-done.65, ...), kind=kOutput, calls=%fused_computation.79 | convolution fusion | flops 4316984320 | bytes 18894848 | tf_op jit(solution)/shard_map/dot_general | solution.py:24
  295.9 7.4 %convert_reduce_fusion.2 = (f32[16,64]{1,0:T(8,128)S(1)}, bf16[16,64,512]{2,1,0:T(8,128)(2,1)}) fusion(bf16[512,16,64]{0,2,1:T(8,128)(2,1)} %bitcast.278, bf16[16,512,512]{1,2,0:T(8,128)(2,1)} %copy-done), kind=kOutput, calls=%fused_computation.80 | convolution fusion | flops 538442752 | bytes 10489856 | tf_op jit(solution)/shard_map/hqk,qhd->khd/dot_general | solution.py:189
  303.3 9.2 %fusion.1 = (f32[16,512]{1,0:T(8,128)S(1)}, f32[16,512,512]{1,2,0:T(8,128)}) fusion(bf16[16,512,512]{1,2,0:T(8,128)(2,1)} %copy-done, bf16[512,16,64]{0,2,1:T(8,128)(2,1)S(1)} %bitcast.279, bf16[512,16,64]{0,2,1:T(8,128)(2,1)S(1)} %bitcast.275), kind=kOutput, calls=%fused_computation.3 | convolution fusion | flops 549445632 | bytes 27295744 | tf_op jit(solution)/shard_map/qhd,khd->hqk/dot_general | solution.py:183
  312.5 7.8 %reshape.309 = bf16[512,2,2,1024]{3,2,1,0:T(2,128)(2,1)} reshape(bf16[512,4096]{1,0:T(8,128)(2,1)} %get-tuple-element.113) | data formatting | bytes 8388608 | tf_op jit(solution)/shard_map/reshape | solution.py:168
  320.3 7.8 %reshape.307 = bf16[512,2,2,1024]{3,2,1,0:T(2,128)(2,1)} reshape(bf16[512,4096]{1,0:T(8,128)(2,1)} %copy-done.26) | data formatting | bytes 8388608 | tf_op jit(solution)/shard_map/reshape | solution.py:168
  328.1 11.7 %fusion.2 = bf16[16,512,512]{1,2,0:T(8,128)(2,1)S(1)} fusion(f32[16,512,512]{1,2,0:T(8,128)} %get-tuple-element.119, f32[16,512]{1,0:T(8,128)S(1)} %get-tuple-element.118, f32[16,512,512]{1,2,0:T(8,128)} %get-tuple-element.110, f32[16,512]{1,0:T(8,128)S(1)} %get-tuple-element.109), kind=kLoop, calls=%fused_computation.4 | loop fusion | flops 25165824 | bytes 42008576 | tf_op jit(solution)/shard_map/convert_element_type | solution.py:186
  345.4 39.8 %psum.7 = f32[96,128]{1,0:T(8,128)S(1)} all-reduce(f32[96,128]{1,0:T(8,128)S(1)} %bitcast.325), channel_id=1, replica_groups=mesh['dp'=8,'ctx'=2,'tp'=2] {'dp','ctx','tp'}, use_global_device_ids=true, to_apply=%region_20.21 | all-reduce | flops 12288 | bytes 98304 | tf_op jit(solution)/shard_map/psum | solution.py:208
  385.2 11.1 %constant_dynamic-slice_fusion.7 = (bf16[512,2,1,1024]{3,2,1,0:T(2,128)(2,1)}, bf16[512,2,1,1024]{3,2,1,0:T(2,128)(2,1)S(1)}) fusion(bf16[512,2,2,1024]{3,2,1,0:T(2,128)(2,1)} %reshape.309, s32[]{:T(128)S(6)} %select_n.229, s32[]{:T(128)S(6)} %select_n.230), kind=kLoop, calls=%fused_computation.250 | loop fusion | bytes 8388616 | tf_op jit(solution)/shard_map/jit(dynamic_index_in_dim)/dynamic_slice | solution.py:46
  398.9 9.8 %constant_dynamic-slice_fusion.14 = (bf16[512,2,1,1024]{3,2,1,0:T(2,128)(2,1)}, bf16[512,2,1,1024]{3,2,1,0:T(2,128)(2,1)}) fusion(bf16[512,2,2,1024]{3,2,1,0:T(2,128)(2,1)S(1)} %copy-done.1, s32[]{:T(128)S(6)} %select_n.229, s32[]{:T(128)S(6)} %select_n.230), kind=kLoop, calls=%fused_computation.257 | loop fusion | bytes 8388616 | tf_op jit(solution)/shard_map/jit(dynamic_index_in_dim)/dynamic_slice | solution.py:46
  421.3 10.5 %copy.151 = bf16[512,2,1,1024]{0,3,1,2:T(8,128)(2,1)} copy(bf16[512,2,1,1024]{3,2,1,0:T(2,128)(2,1)} %get-tuple-element.45) | data formatting | bytes 4194304
  436.5 10.8 %copy.147 = bf16[512,2,1,1024]{0,3,1,2:T(8,128)(2,1)} copy(bf16[512,2,1,1024]{3,2,1,0:T(2,128)(2,1)} %get-tuple-element.49) | data formatting | bytes 4194304
  484.3 12.6 %collective-permute-done.4 = bf16[2,256,1024]{2,1,0:T(8,128)(2,1)} collective-permute-done((bf16[2,256,1024]{2,1,0:T(8,128)(2,1)S(1)}, bf16[2,256,1024]{2,1,0:T(8,128)(2,1)}, u32[]{:S(2)}, u32[]{:S(2)}) %collective-permute-start.4) | collective-permute-done | bytes 1048608 | tf_op jit(solution)/shard_map/ppermute | solution.py:42
  500.1 19.0 %collective-permute-done.2 = bf16[2,256,1024]{2,1,0:T(8,128)(2,1)} collective-permute-done((bf16[2,256,1024]{2,1,0:T(8,128)(2,1)S(1)}, bf16[2,256,1024]{2,1,0:T(8,128)(2,1)}, u32[]{:S(2)}, u32[]{:S(2)}) %collective-permute-start.2) | collective-permute-done | bytes 1048608 | tf_op jit(solution)/shard_map/ppermute | solution.py:42
  529.9 6.8 fusion.24
  549.4 5.7 constant_dynamic-slice_fusion.5
  561.0 6.9 fusion.27
  598.9 5.7 constant_dynamic-slice_fusion.12
  607.6 6.8 collective-permute-done.16
  624.6 6.2 collective-permute-done.23
  635.2 5.5 collective-permute-done.21
  670.7 10.4 %collective-permute-done.36 = bf16[128,1024]{1,0:T(8,128)(2,1)S(1)} collective-permute-done((bf16[128,1024]{1,0:T(8,128)(2,1)S(1)}, bf16[128,1024]{1,0:T(8,128)(2,1)S(1)}, u32[]{:S(2)}, u32[]{:S(2)}) %collective-permute-start.36) | collective-permute-done | bytes 262176 | tf_op jit(solution)/shard_map/ppermute | solution.py:83
  682.7 13.1 %collective-permute-done.26 = bf16[128,1024]{1,0:T(8,128)(2,1)S(1)} collective-permute-done((bf16[128,1024]{1,0:T(8,128)(2,1)S(1)}, bf16[128,1024]{1,0:T(8,128)(2,1)S(1)}, u32[]{:S(2)}, u32[]{:S(2)}) %collective-permute-start.26) | collective-permute-done | bytes 262176 | tf_op jit(solution)/shard_map/ppermute | solution.py:83
  (376 shorter events, 254.9 us)
Async XLA Ops:
  7.2 85.0 %all-gather.6.cloned.1.call-start = ((), (), s32[]{:S(2)}) async-start(), calls=%async_computation | async-start | bytes 8650752 | tf_op jit(solution)/shard_map/all_gather | solution.py:54
  11.8 159.3 %all-gather.8.cloned.1.call-start = ((), (), s32[]{:S(2)}) async-start(), calls=%async_computation.1 | async-start | bytes 8650752 | tf_op jit(solution)/shard_map/all_gather | solution.py:54
  13.7 236.4 %all-gather.10.cloned.1.call-start = ((), (), s32[]{:S(2)}) async-start(), calls=%async_computation.2 | async-start | bytes 8650752 | tf_op jit(solution)/shard_map/all_gather | solution.py:54
  33.3 415.0 %collective-permute-start.5 = (bf16[512,1024]{1,0:T(8,128)(2,1)}, bf16[512,1024]{1,0:T(8,128)(2,1)}, u32[]{:S(2)}, u32[]{:S(2)}) collective-permute-start(bf16[512,1024]{1,0:T(8,128)(2,1)} %pad_maximum_fusion.27), channel_id=1, source_target_pairs={{0,2},{2,0},{1,3},{3,1},{4,6},{6,4},{5,7},{7,5},{8,10},{10,8},{9,1... | collective-permute-start | bytes 3145736 | tf_op jit(solution)/shard_map/ppermute | solution.py:42
  344.9 127.8 %collective-permute-start.9 = (bf16[512,1024]{1,0:T(8,128)(2,1)}, bf16[512,1024]{1,0:T(8,128)(2,1)}, u32[]{:S(2)}, u32[]{:S(2)}) collective-permute-start(bf16[512,1024]{1,0:T(8,128)(2,1)} %convert_element_type.356), channel_id=1, source_target_pairs={{0,2},{2,0},{1,3},{3,1},{4,6},{6,4},{5,7},{7,5},{8,10},{10,8},{9,1... | collective-permute-start | bytes 3145736 | tf_op jit(solution)/shard_map/ppermute | solution.py:42
  398.8 125.2 %collective-permute-start.30 = (bf16[512,2,1024]{2,0,1:T(8,128)(2,1)}, bf16[512,2,1024]{2,0,1:T(8,128)(2,1)}, u32[]{:S(2)}, u32[]{:S(2)}) collective-permute-start(bf16[512,2,1024]{2,0,1:T(8,128)(2,1)} %bitcast.268), channel_id=1, source_target_pairs={{0,2},{2,0},{1,3},{3,1},{4,6},{6,4},{5,7},{7,5},{8,10},{10,8},{9,1... | collective-permute-start | bytes 6291464 | tf_op jit(solution)/shard_map/ppermute | solution.py:42
  409.7 38.6 %collective-permute-start.6 = (bf16[512,2,256]{0,2,1:T(8,128)(2,1)}, bf16[512,2,256]{0,2,1:T(8,128)(2,1)}, u32[]{:S(2)}, u32[]{:S(2)}) collective-permute-start(bf16[512,2,256]{0,2,1:T(8,128)(2,1)} %get-tuple-element.76), channel_id=1, source_target_pairs={{0,2},{2,0},{1,3},{3,1},{4,6},{6,4},{5,7},{7,5},{8,10},{10,8},{9,1... | collective-permute-start | bytes 1572872 | tf_op jit(solution)/shard_map/ppermute | solution.py:42
  411.3 41.3 %collective-permute-start.7 = (bf16[512,2,256]{0,2,1:T(8,128)(2,1)}, bf16[512,2,256]{0,2,1:T(8,128)(2,1)}, u32[]{:S(2)}, u32[]{:S(2)}) collective-permute-start(bf16[512,2,256]{0,2,1:T(8,128)(2,1)} %get-tuple-element.78), channel_id=1, source_target_pairs={{0,2},{2,0},{1,3},{3,1},{4,6},{6,4},{5,7},{7,5},{8,10},{10,8},{9,1... | collective-permute-start | bytes 1572872 | tf_op jit(solution)/shard_map/ppermute | solution.py:42
  466.7 63.2 %collective-permute-start.29 = (bf16[512,1024]{1,0:T(8,128)(2,1)}, bf16[512,1024]{1,0:T(8,128)(2,1)}, u32[]{:S(2)}, u32[]{:S(2)}) collective-permute-start(bf16[512,1024]{1,0:T(8,128)(2,1)} %convert_element_type.353), channel_id=1, source_target_pairs={{0,2},{2,0},{1,3},{3,1},{4,6},{6,4},{5,7},{7,5},{8,10},{10,8},{9,1... | collective-permute-start | bytes 3145736 | tf_op jit(solution)/shard_map/ppermute | solution.py:42
  468.9 92.1 %collective-permute-start.19 = (bf16[512,1024]{1,0:T(8,128)(2,1)}, bf16[512,1024]{1,0:T(8,128)(2,1)}, u32[]{:S(2)}, u32[]{:S(2)}) collective-permute-start(bf16[512,1024]{1,0:T(8,128)(2,1)} %fusion.53), channel_id=1, source_target_pairs={{0,2},{2,0},{1,3},{3,1},{4,6},{6,4},{5,7},{7,5},{8,10},{10,8},{9,1... | collective-permute-start | bytes 3145736 | tf_op jit(solution)/shard_map/ppermute | solution.py:42
  470.4 26.5 %collective-permute-start.4 = (bf16[2,256,1024]{2,1,0:T(8,128)(2,1)S(1)}, bf16[2,256,1024]{2,1,0:T(8,128)(2,1)}, u32[]{:S(2)}, u32[]{:S(2)}) collective-permute-start(bf16[2,256,1024]{2,1,0:T(8,128)(2,1)S(1)} %maximum_select_fusion.3), channel_id=1, source_target_pairs={{0,1},{1,0},{2,3},{3,2},{4,5},{5,4},{6,7},{7,6},{8,9},{9,8},{10,11... | collective-permute-start | bytes 3145736 | tf_op jit(solution)/shard_map/ppermute | solution.py:42
  472.8 46.4 %collective-permute-start.2 = (bf16[2,256,1024]{2,1,0:T(8,128)(2,1)S(1)}, bf16[2,256,1024]{2,1,0:T(8,128)(2,1)}, u32[]{:S(2)}, u32[]{:S(2)}) collective-permute-start(bf16[2,256,1024]{2,1,0:T(8,128)(2,1)S(1)} %maximum_select_fusion.2), channel_id=1, source_target_pairs={{0,1},{1,0},{2,3},{3,2},{4,5},{5,4},{6,7},{7,6},{8,9},{9,8},{10,11... | collective-permute-start | bytes 3145736 | tf_op jit(solution)/shard_map/ppermute | solution.py:42
  496.9 59.5 %collective-permute-start.20 = (bf16[512,2,1024]{2,0,1:T(8,128)(2,1)}, bf16[512,2,1024]{2,0,1:T(8,128)(2,1)}, u32[]{:S(2)}, u32[]{:S(2)}) collective-permute-start(bf16[512,2,1024]{2,0,1:T(8,128)(2,1)} %bitcast.269), channel_id=1, source_target_pairs={{0,2},{2,0},{1,3},{3,1},{4,6},{6,4},{5,7},{7,5},{8,10},{10,8},{9,1... | collective-permute-start | bytes 6291464 | tf_op jit(solution)/shard_map/ppermute | solution.py:42
  519.1 48.8 %collective-permute-start.13 = (bf16[2,128,2,1024]{3,1,0,2:T(8,128)(2,1)}, bf16[2,128,2,1024]{3,1,0,2:T(8,128)(2,1)}, u32[]{:S(2)}, u32[]{:S(2)}) collective-permute-start(bf16[2,128,2,1024]{3,1,0,2:T(8,128)(2,1)} %dynamic-slice_bitcast_fusion), channel_id=1, source_target_pairs={{0,4},{4,0},{8,12},{12,8},{16,20},{20,16},{24,28},{28,24},{1,5},{5... | collective-permute-start | bytes 3145736 | tf_op jit(solution)/shard_map/ppermute | solution.py:72
  524.0 48.0 %collective-permute-start.11 = (bf16[2,2,128,1024]{3,2,1,0:T(8,128)(2,1)}, bf16[2,2,128,1024]{3,2,1,0:T(8,128)(2,1)}, u32[]{:S(2)}, u32[]{:S(2)}) collective-permute-start(bf16[2,2,128,1024]{3,2,1,0:T(8,128)(2,1)} %dynamic-slice_bitcast_fusion.1), channel_id=1, source_target_pairs={{0,1},{1,0},{2,3},{3,2},{4,5},{5,4},{6,7},{7,6},{8,9},{9,8},{10,11... | collective-permute-start | bytes 3145736 | tf_op jit(solution)/shard_map/ppermute | solution.py:42
  545.4 71.0 %collective-permute-start.33 = (bf16[2,128,2,1024]{3,1,0,2:T(8,128)(2,1)}, bf16[2,128,2,1024]{3,1,0,2:T(8,128)(2,1)}, u32[]{:S(2)}, u32[]{:S(2)}) collective-permute-start(bf16[2,128,2,1024]{3,1,0,2:T(8,128)(2,1)} %bitcast.270), channel_id=1, source_target_pairs={{0,4},{4,0},{8,12},{12,8},{16,20},{20,16},{24,28},{28,24},{1,5},{5... | collective-permute-start | bytes 3145736 | tf_op jit(solution)/shard_map/ppermute | solution.py:72
  556.4 63.9 %collective-permute-start.31 = (bf16[2,2,128,1024]{3,2,0,1:T(8,128)(2,1)}, bf16[2,2,128,1024]{3,2,0,1:T(8,128)(2,1)}, u32[]{:S(2)}, u32[]{:S(2)}) collective-permute-start(bf16[2,2,128,1024]{3,2,0,1:T(8,128)(2,1)} %bitcast.271), channel_id=1, source_target_pairs={{0,1},{1,0},{2,3},{3,2},{4,5},{5,4},{6,7},{7,6},{8,9},{9,8},{10,11... | collective-permute-start | bytes 3145736 | tf_op jit(solution)/shard_map/ppermute | solution.py:42
  570.6 21.2 %collective-permute-start.14 = (bf16[2,128,1024]{2,1,0:T(8,128)(2,1)}, bf16[2,128,1024]{2,1,0:T(8,128)(2,1)}, u32[]{:S(2)}, u32[]{:S(2)}) collective-permute-start(bf16[2,128,1024]{2,1,0:T(8,128)(2,1)} %dynamic-slice_bitcast_fusion.6), channel_id=1, source_target_pairs={{0,1},{1,0},{2,3},{3,2},{4,5},{5,4},{6,7},{7,6},{8,9},{9,8},{10,11... | collective-permute-start | bytes 1572872 | tf_op jit(solution)/shard_map/ppermute | solution.py:42
  574.6 18.6 %collective-permute-start.12 = (bf16[2,128,1024]{2,1,0:T(8,128)(2,1)}, bf16[2,128,1024]{2,1,0:T(8,128)(2,1)}, u32[]{:S(2)}, u32[]{:S(2)}) collective-permute-start(bf16[2,128,1024]{2,1,0:T(8,128)(2,1)} %dynamic-slice_bitcast_fusion.7), channel_id=1, source_target_pairs={{0,4},{4,0},{8,12},{12,8},{16,20},{20,16},{24,28},{28,24},{1,5},{5... | collective-permute-start | bytes 1572872 | tf_op jit(solution)/shard_map/ppermute | solution.py:75
  595.6 18.8 %collective-permute-start.16 = (bf16[128,1024]{1,0:T(8,128)(2,1)S(1)}, bf16[128,1024]{1,0:T(8,128)(2,1)S(1)}, u32[]{:S(2)}, u32[]{:S(2)}) collective-permute-start(bf16[128,1024]{1,0:T(8,128)(2,1)S(1)} %get-tuple-element.73), channel_id=1, source_target_pairs={{0,16},{4,20},{8,24},{12,28},{16,0},{20,4},{24,8},{28,12},{1,17},{... | collective-permute-start | bytes 786440 | tf_op jit(solution)/shard_map/ppermute | solution.py:83
  606.1 24.7 %collective-permute-start.23 = (bf16[2,128,2,1024]{3,1,0,2:T(8,128)(2,1)}, bf16[2,128,2,1024]{3,1,0,2:T(8,128)(2,1)S(1)}, u32[]{:S(2)}, u32[]{:S(2)}) collective-permute-start(bf16[2,128,2,1024]{3,1,0,2:T(8,128)(2,1)} %bitcast.272), channel_id=1, source_target_pairs={{0,4},{4,0},{8,12},{12,8},{16,20},{20,16},{24,28},{28,24},{1,5},{5... | collective-permute-start | bytes 3145736 | tf_op jit(solution)/shard_map/ppermute | solution.py:72
  614.4 26.4 %collective-permute-start.21 = (bf16[2,2,128,1024]{3,2,0,1:T(8,128)(2,1)}, bf16[2,2,128,1024]{3,2,0,1:T(8,128)(2,1)}, u32[]{:S(2)}, u32[]{:S(2)}) collective-permute-start(bf16[2,2,128,1024]{3,2,0,1:T(8,128)(2,1)} %bitcast.273), channel_id=1, source_target_pairs={{0,1},{1,0},{2,3},{3,2},{4,5},{5,4},{6,7},{7,6},{8,9},{9,8},{10,11... | collective-permute-start | bytes 3145736 | tf_op jit(solution)/shard_map/ppermute | solution.py:42
  616.2 28.8 %collective-permute-start.18 = (f32[64,1024]{1,0:T(8,128)}, f32[64,1024]{1,0:T(8,128)}, u32[]{:S(2)}, u32[]{:S(2)}) collective-permute-start(f32[64,1024]{1,0:T(8,128)} %get-tuple-element.98), channel_id=1, source_target_pairs={{0,2},{2,0},{1,3},{3,1},{4,6},{6,4},{5,7},{7,5},{8,10},{10,8},{9,1... | collective-permute-start | bytes 786440 | tf_op jit(solution)/shard_map/ppermute | solution.py:42
  619.0 33.0 %collective-permute-start.34 = (bf16[2,128,1024]{2,1,0:T(8,128)(2,1)}, bf16[2,128,1024]{2,1,0:T(8,128)(2,1)}, u32[]{:S(2)}, u32[]{:S(2)}) collective-permute-start(bf16[2,128,1024]{2,1,0:T(8,128)(2,1)} %dynamic-slice_bitcast_fusion.2), channel_id=1, source_target_pairs={{0,1},{1,0},{2,3},{3,2},{4,5},{5,4},{6,7},{7,6},{8,9},{9,8},{10,11... | collective-permute-start | bytes 1572872 | tf_op jit(solution)/shard_map/ppermute | solution.py:42
  623.1 30.2 %collective-permute-start.32 = (bf16[2,128,1024]{2,1,0:T(8,128)(2,1)}, bf16[2,128,1024]{2,1,0:T(8,128)(2,1)}, u32[]{:S(2)}, u32[]{:S(2)}) collective-permute-start(bf16[2,128,1024]{2,1,0:T(8,128)(2,1)} %dynamic-slice_bitcast_fusion.3), channel_id=1, source_target_pairs={{0,4},{4,0},{8,12},{12,8},{16,20},{20,16},{24,28},{28,24},{1,5},{5... | collective-permute-start | bytes 1572872 | tf_op jit(solution)/shard_map/ppermute | solution.py:75
  634.4 26.5 %collective-permute-start.24 = (bf16[2,128,1024]{2,1,0:T(8,128)(2,1)}, bf16[2,128,1024]{2,1,0:T(8,128)(2,1)}, u32[]{:S(2)}, u32[]{:S(2)}) collective-permute-start(bf16[2,128,1024]{2,1,0:T(8,128)(2,1)} %dynamic-slice_bitcast_fusion.4), channel_id=1, source_target_pairs={{0,1},{1,0},{2,3},{3,2},{4,5},{5,4},{6,7},{7,6},{8,9},{9,8},{10,11... | collective-permute-start | bytes 1572872 | tf_op jit(solution)/shard_map/ppermute | solution.py:42
  643.4 18.7 %collective-permute-start.22 = (bf16[2,128,1024]{2,1,0:T(8,128)(2,1)}, bf16[2,128,1024]{2,1,0:T(8,128)(2,1)}, u32[]{:S(2)}, u32[]{:S(2)}) collective-permute-start(bf16[2,128,1024]{2,1,0:T(8,128)(2,1)} %dynamic-slice_bitcast_fusion.5), channel_id=1, source_target_pairs={{0,4},{4,0},{8,12},{12,8},{16,20},{20,16},{24,28},{28,24},{1,5},{5... | collective-permute-start | bytes 1572872 | tf_op jit(solution)/shard_map/ppermute | solution.py:75
  657.5 23.6 %collective-permute-start.36 = (bf16[128,1024]{1,0:T(8,128)(2,1)S(1)}, bf16[128,1024]{1,0:T(8,128)(2,1)S(1)}, u32[]{:S(2)}, u32[]{:S(2)}) collective-permute-start(bf16[128,1024]{1,0:T(8,128)(2,1)S(1)} %get-tuple-element.67), channel_id=1, source_target_pairs={{0,16},{4,20},{8,24},{12,28},{16,0},{20,4},{24,8},{28,12},{1,17},{... | collective-permute-start | bytes 786440 | tf_op jit(solution)/shard_map/ppermute | solution.py:83
  660.9 20.3 %collective-permute-start.37 = (bf16[128,1024]{1,0:T(8,128)(2,1)S(1)}, bf16[128,1024]{1,0:T(8,128)(2,1)S(1)}, u32[]{:S(2)}, u32[]{:S(2)}) collective-permute-start(bf16[128,1024]{1,0:T(8,128)(2,1)S(1)} %get-tuple-element.68), channel_id=1, source_target_pairs={{0,24},{4,28},{8,0},{12,4},{16,8},{20,12},{24,16},{28,20},{1,25},{... | collective-permute-start | bytes 786440 | tf_op jit(solution)/shard_map/ppermute | solution.py:83
  663.7 18.9 %collective-permute-start.25 = (bf16[128,1024]{1,0:T(8,128)(2,1)S(1)}, bf16[128,1024]{1,0:T(8,128)(2,1)S(1)}, u32[]{:S(2)}, u32[]{:S(2)}) collective-permute-start(bf16[128,1024]{1,0:T(8,128)(2,1)S(1)} %get-tuple-element.69), channel_id=1, source_target_pairs={{0,8},{4,12},{8,16},{12,20},{16,24},{20,28},{24,0},{28,4},{1,9},{5... | collective-permute-start | bytes 786440 | tf_op jit(solution)/shard_map/ppermute | solution.py:83
  665.8 30.0 %collective-permute-start.26 = (bf16[128,1024]{1,0:T(8,128)(2,1)S(1)}, bf16[128,1024]{1,0:T(8,128)(2,1)S(1)}, u32[]{:S(2)}, u32[]{:S(2)}) collective-permute-start(bf16[128,1024]{1,0:T(8,128)(2,1)S(1)} %get-tuple-element.70), channel_id=1, source_target_pairs={{0,16},{4,20},{8,24},{12,28},{16,0},{20,4},{24,8},{28,12},{1,17},{... | collective-permute-start | bytes 786440 | tf_op jit(solution)/shard_map/ppermute | solution.py:83
  667.8 28.0 %collective-permute-start.27 = (bf16[128,1024]{1,0:T(8,128)(2,1)S(1)}, bf16[128,1024]{1,0:T(8,128)(2,1)S(1)}, u32[]{:S(2)}, u32[]{:S(2)}) collective-permute-start(bf16[128,1024]{1,0:T(8,128)(2,1)S(1)} %get-tuple-element.71), channel_id=1, source_target_pairs={{0,24},{4,28},{8,0},{12,4},{16,8},{20,12},{24,16},{28,20},{1,25},{... | collective-permute-start | bytes 786440 | tf_op jit(solution)/shard_map/ppermute | solution.py:83
  (85 other events, 807.8 us)
Sparse Core Ops, SparseCore 0:
  12.0 80.1 all-gather.5
  95.0 76.0 all-gather.7
  174.0 76.0 all-gather.9

commit v2 on v1

v2 whole, which is shorter than its diff:
```python
import functools

import jax
import jax.numpy as jnp
from jax import lax
from jax.experimental import pallas as pl
from jax.experimental.pallas import tpu as pltpu
from jax.sharding import PartitionSpec as P

HEAD_DIM = 64
LANES = 2 * HEAD_DIM

epsilon = 1e-12
root_half = 0.7071067811865476
inv_root_two_pi = 0.3989422804014327
bf16 = jnp.bfloat16
f32 = jnp.float32


def dot(left, right, left_dim, right_dim):
    return lax.dot_general(left, right, (((left_dim,), (right_dim,)), ((), ())), preferred_element_type=f32)


def norm_forward(values, gain, shift):
    centre = values - jnp.mean(values, axis=-1, keepdims=True)
    inverse = lax.rsqrt(jnp.mean(centre * centre, axis=-1, keepdims=True) + epsilon)
    normed = centre * inverse
    return (normed * gain + shift, normed, inverse)


def norm_backward(upstream, normed, inverse, gain):
    scaled = upstream * gain
    inner = scaled - jnp.mean(scaled, axis=-1, keepdims=True)
    inner = inner - normed * jnp.mean(scaled * normed, axis=-1, keepdims=True)
    return (inner * inverse, jnp.sum(upstream * normed, axis=0), jnp.sum(upstream, axis=0))


def swap(values, axis):
    return lax.ppermute(values, axis, [(0, 1), (1, 0)])


def swap_x(values):
    return lax.ppermute(values, "dp", [(i, i ^ 1) for i in range(8)])


def shift_z(values, step):
    return lax.ppermute(values, "dp", [(i, (i + 2 * step) % 8) for i in range(8)])


def take(values, index, axis=0):
    return lax.dynamic_index_in_dim(values, index, axis, keepdims=False)


def add(left, right):
    return (left.astype(f32) + right.astype(f32)).astype(bf16)


def order(index, mine, other, axis):
    return jnp.where(index == 0, jnp.concatenate([mine, other], axis), jnp.concatenate([other, mine], axis))


def assemble_kernel(cuts, place, one, one_y, two, two_x, *rest):
    outs, sems = rest[: len(cuts)], rest[len(cuts)]
    z, x = place[0], place[1]
    rows = one.shape[2]
    for k in range(4):
        for far_x in range(2):
            block = lax.rem(z + 4 - k, 4) * 2 + lax.rem(x + far_x, 2)
            at = pl.ds(pl.multiple_of(block * rows, rows), rows)
            for far_t in range(2):
                if k < 2:
                    source = (one_y if far_t else one).at[far_x, k]
                else:
                    source = (two_x if far_x else two).at[far_t, k - 2]
                for n, (start, size) in enumerate(cuts):
                    pltpu.make_async_copy(
                        source.at[:, start : start + size],
                        outs[n].at[at, far_t * size : far_t * size + size],
                        sems.at[n],
                    ).start()
    for n in range(len(cuts)):
        pltpu.make_async_copy(outs[n], outs[n], sems.at[n]).wait()


def gather_weights(piece, cuts, place, dp_count):
    rows, cols = piece.shape
    total = dp_count * rows
    if dp_count != 8:
        t = lax.axis_index("tp")
        both = lax.all_gather(piece, ("tp", "dp"), axis=0, tiled=True).reshape(2, total, cols)
        first, second = take(both, t), take(both, 1 - t)
        return [
            jnp.concatenate([first[:, s : s + n], second[:, s : s + n]], 1) for s, n in cuts
        ]
    line = [piece] + [shift_z(piece, k) for k in range(1, 4)]
    one, two = jnp.stack(line[:2]), jnp.stack(line[2:])
    one_x, two_y = swap_x(one), swap(two, "tp")
    one, two = jnp.stack([one, one_x]), jnp.stack([two, two_y])
    one_y, two_x = swap(one, "tp"), swap_x(two)
    anyspace = pl.BlockSpec(memory_space=pl.ANY)


    return pl.pallas_call(
        functools.partial(assemble_kernel, cuts),
        out_shape=[jax.ShapeDtypeStruct((total, 2 * n), bf16) for _, n in cuts],
        in_specs=[pl.BlockSpec(memory_space=pltpu.SMEM)] + [anyspace] * 4,
        out_specs=[anyspace] * len(cuts),
        scratch_shapes=[pltpu.SemaphoreType.DMA((len(cuts),))],
        name="assemble",
    )(place, one, one_y, two, two_x)


def attend_kernel(qkv, seg_keys, seg_queries, context, probs, bias):
    quarter = qkv.shape[1] // 3

    @pl.when(pl.program_id(0) == 0)
    def _():
        bias[...] = jnp.where(seg_keys[...] == seg_queries[...], 0.0, -1000000000.0)

    low = lax.broadcasted_iota(jnp.int32, (1, LANES), 1) < HEAD_DIM
    for pair in range(quarter // LANES):
        cols = slice(pair * LANES, pair * LANES + LANES)
        query = qkv[:, cols] * 0.125
        key = qkv[:, quarter + pair * LANES : quarter + pair * LANES + LANES]
        value_t = qkv[:, 2 * quarter + pair * LANES : 2 * quarter + pair * LANES + LANES].T
        parts = []
        for h in range(2):
            mine = jnp.where(low if h == 0 else ~low, query, jnp.zeros_like(query))
            scores = dot(key, mine, 1, 1) + bias[...]
            raised = jnp.exp(scores - jnp.max(scores, axis=0, keepdims=True))
            prob = (raised * (1.0 / jnp.sum(raised, axis=0, keepdims=True))).astype(bf16)
            probs[2 * pair + h] = prob
            parts.append(dot(value_t[h * HEAD_DIM : (h + 1) * HEAD_DIM], prob, 1, 0))
        context[:, cols] = jnp.concatenate(parts, 0).T.astype(bf16)


def attend(qkv, seg):
    rows, cols = qkv.shape
    half = cols // 2
    quarter = half // 3
    heads = quarter // HEAD_DIM
    return pl.pallas_call(
        attend_kernel,
        grid=(2,),
        out_shape=[jax.ShapeDtypeStruct((rows, 2 * quarter), bf16), jax.ShapeDtypeStruct((2 * heads, rows, rows), bf16)],
        in_specs=[
            pl.BlockSpec((rows, half), lambda i: (0, i)),
            pl.BlockSpec((rows, 1), lambda i: (0, 0)),
            pl.BlockSpec((1, rows), lambda i: (0, 0)),
        ],
        out_specs=[pl.BlockSpec((rows, quarter), lambda i: (0, i)), pl.BlockSpec((heads, rows, rows), lambda i: (i, 0, 0))],
        scratch_shapes=[pltpu.VMEM((rows, rows), f32)],
        compiler_params=pltpu.CompilerParams(vmem_limit_bytes=48 << 20),
        cost_estimate=pl.CostEstimate(flops=12_000_000_000, bytes_accessed=8 << 20, transcendentals=2 << 20),
        name="attend",
    )(qkv, seg.reshape(rows, 1), seg.reshape(1, rows))


def attend_back_kernel(qkv, probs, upstream, grads, sums):
    quarter = qkv.shape[1] // 3
    low = lax.broadcasted_iota(jnp.int32, (1, LANES), 1) < HEAD_DIM
    for pair in range(quarter // LANES):
        cols = [slice(n * quarter + pair * LANES, n * quarter + pair * LANES + LANES) for n in range(3)]
        query, key, value = (qkv[:, c] for c in cols)
        key_t = key.T
        above = upstream[:, cols[0]]
        grad_q, grad_k, grad_v = [], [], []
        for h in range(2):
            mine = jnp.where(low if h == 0 else ~low, above, jnp.zeros_like(above))
            grad_p = dot(value, mine, 1, 1)
            prob_low = probs[2 * pair + h]
            prob = prob_low.astype(f32)
            weighted = prob * grad_p
            inner = jnp.sum(weighted, axis=0, keepdims=True)
            grad_s = (weighted - prob * inner).astype(bf16)
            grad_k.append(dot(grad_s, query, 1, 0))
            grad_v.append(dot(prob_low, above, 1, 0))
            grad_q.append(dot(key_t[h * HEAD_DIM : (h + 1) * HEAD_DIM], grad_s, 1, 0))
        out_q = (jnp.concatenate(grad_q, 0) * 0.125).T.astype(bf16)
        out_v = jnp.where(low, grad_v[0], grad_v[1]).astype(bf16)
        grads[:, cols[0]] = out_q
        grads[:, cols[1]] = (jnp.where(low, grad_k[0], grad_k[1]) * 0.125).astype(bf16)
        grads[:, cols[2]] = out_v
        for n, out in ((0, out_q), (1, out_v)):
            total = jnp.sum(out.astype(f32), axis=0, keepdims=True)
            sums[0, n, :, cols[0]] = jnp.broadcast_to(total, (8, LANES))


def attend_back(qkv, probs, upstream):
    rows, cols = qkv.shape
    half = cols // 2
    quarter = half // 3
    heads = quarter // HEAD_DIM
    return pl.pallas_call(
        attend_back_kernel,
        grid=(2,),
        out_shape=[jax.ShapeDtypeStruct((rows, cols), bf16), jax.ShapeDtypeStruct((2, 2, 8, quarter), f32)],
        in_specs=[
            pl.BlockSpec((rows, half), lambda i: (0, i)),
            pl.BlockSpec((heads, rows, rows), lambda i: (i, 0, 0)),
            pl.BlockSpec((rows, quarter), lambda i: (0, i)),
        ],
        out_specs=[pl.BlockSpec((rows, half), lambda i: (0, i)), pl.BlockSpec((1, 2, 8, quarter), lambda i: (i, 0, 0, 0))],
        compiler_params=pltpu.CompilerParams(vmem_limit_bytes=48 << 20),
        cost_estimate=pl.CostEstimate(flops=20_000_000_000, bytes_accessed=8 << 20, transcendentals=0),
        name="attend_back",
    )(qkv, probs, upstream)


def scatter_sum(grad, dp_count):
    rows, _, cols = grad.shape
    if dp_count != 8:
        t = lax.axis_index("tp")
        mine = add(grad[:, 0], swap(grad[:, 1], "tp"))
        return lax.psum_scatter(mine, "dp", scatter_dimension=0, tiled=True).astype(f32)
    d = lax.axis_index("dp")
    x, z = d % 2, d // 2
    blocks = grad.reshape(2, 2, 2, rows // 8, 2, cols)
    first, second = blocks[0], blocks[1]
    got = swap(first[:, :, :, 1], "tp")
    got_b = swap_x(take(second, 1 - x, 1))
    first = add(first[:, :, :, 0], got)
    second = add(take(second, x, 1), got_b)
    got = swap_x(take(first, 1 - x, 1))
    got_b = swap(second[:, :, 1], "tp")
    first = add(take(first, x, 1), got)
    second = add(second[:, :, 0], got_b)
    line = jnp.concatenate([first, second], axis=0)
    total = take(line, z).astype(f32)
    for step in range(1, 4):
        total = total + shift_z(take(line, (z + step) % 4), step).astype(f32)
    return total


def body(dp_count, tokens, segments, query_weight, key_weight, value_weight, out_weight, up_weight, down_weight, query_bias, value_bias, out_bias, up_bias, down_bias, attn_gain, attn_shift, mlp_gain, mlp_shift, cotangent):
    c = lax.axis_index("ctx")
    t = lax.axis_index("tp")
    d = lax.axis_index("dp")
    place = jnp.stack([d // 2, d % 2]).astype(jnp.int32)
    half, width = tokens.shape[1], tokens.shape[2]
    rows = 2 * half
    inner = 2 * query_bias.shape[0]
    ff = 2 * up_bias.shape[0]
    piece_rows = query_weight.shape[0]

    one = jnp.stack([query_weight, key_weight, value_weight, out_weight.T], 1)
    one = one.reshape(piece_rows, 4, 2, -1).transpose(2, 0, 1, 3).reshape(2, piece_rows, -1)
    up = up_weight.reshape(piece_rows, 2, -1).transpose(1, 0, 2)
    down = down_weight.T.reshape(piece_rows, 2, -1).transpose(1, 0, 2)
    packed = jnp.stack([one, up, down], 1).astype(bf16)
    pieces = order(c, take(packed, c), swap(take(packed, 1 - c), "ctx"), 1)
    unit = pieces.shape[2]
    quarter = unit // 4
    whole = ((0, unit),)
    qkv_mine, out_mine = gather_weights(pieces[0], ((0, 3 * quarter), (3 * quarter, quarter)), place, dp_count)
    w_qkv = (qkv_mine, swap(qkv_mine, "ctx"))
    w_out = (out_mine, swap(out_mine, "ctx"))
    (up_mine,) = gather_weights(pieces[1], whole, place, dp_count)
    w_up = (up_mine, swap(up_mine, "ctx"))
    (down_mine,) = gather_weights(pieces[2], whole, place, dp_count)
    w_down = (down_mine, swap(down_mine, "ctx"))

    biases = jnp.concatenate([query_bias, value_bias, up_bias])
    biases = jnp.stack([biases, swap(biases, "tp")])
    hin = inner // 2

    def near(values):
        values = values.reshape(2, 2, -1).transpose(1, 0, 2)
        return jnp.where(c == 0, values, values[::-1])

    bias_q, bias_v, bias_up = near(biases[:, :hin]), near(biases[:, hin : 2 * hin]), near(biases[:, 2 * hin :])
    bias_qkv = jnp.stack([bias_q, jnp.zeros_like(bias_q), bias_v], 2).reshape(2, -1)
    bias_up = bias_up.reshape(2, -1)

    seq = 2 * t + c
    other_seq = 2 * t + 1 - c
    pair_mine = jnp.stack([take(tokens, seq), take(cotangent, seq), take(tokens, other_seq)])
    pair_send = jnp.stack([take(tokens, other_seq), take(cotangent, other_seq), take(tokens, seq)])
    got = swap(pair_send, "ctx")
    flat = jnp.concatenate([pair_mine[0], got[0]], 0)
    flat_far = jnp.concatenate([got[2], pair_mine[2]], 0)
    grad_output = jnp.concatenate([pair_mine[1], got[1]], 0).astype(f32)
    seg = take(segments, seq)
    seg = jnp.where(c == 0, seg, jnp.roll(seg, half))

    qkv = [(dot(flat, w_qkv[r], 1, 0) + bias_qkv[r]).astype(bf16) for r in range(2)]
    attended = [attend(qkv[r], seg) for r in range(2)]
    context = [a[0] for a in attended]
    probs = [a[1] for a in attended]
    resid_one = flat.astype(f32) + dot(context[0], w_out[0], 1, 1) + dot(context[1], w_out[1], 1, 1) + out_bias
    normed_one, unit_one, inverse_one = norm_forward(resid_one, attn_gain, attn_shift)
    normed_low = normed_one.astype(bf16)
    hidden, slope = [], []
    for r in range(2):
        pre = dot(normed_low, w_up[r], 1, 0) + bias_up[r]
        erf_part = lax.erf(pre * root_half)
        hidden.append((0.5 * pre * (1.0 + erf_part)).astype(bf16))
        slope.append((0.5 * (1.0 + erf_part) + pre * jnp.exp(-0.5 * pre * pre) * inv_root_two_pi).astype(bf16))
    mixed = dot(hidden[0], w_down[0], 1, 1) + dot(hidden[1], w_down[1], 1, 1)
    resid_two = normed_one + mixed + down_bias
    output, unit_two, inverse_two = norm_forward(resid_two, mlp_gain, mlp_shift)
    grad_two, mlp_gain_term, mlp_shift_term = norm_backward(grad_output, unit_two, inverse_two, mlp_gain)
    grad_mixed = grad_two.astype(bf16)
    down_bias_term = jnp.sum(grad_two, axis=0)
    grad_pre = [(dot(grad_mixed, w_down[r], 1, 0) * slope[r].astype(f32)).astype(bf16) for r in range(2)]
    up_bias_term = jnp.stack([jnp.sum(g.astype(f32), axis=0) for g in grad_pre])

    def far(values):
        return jnp.concatenate([values, swap(values, "ctx")], 0)

    def mine_and_far(pair):
        return jnp.concatenate([pair[0], swap(pair[1], "ctx")], 0)

    def grads(left, right):
        return dot(left, right, 0, 0).astype(bf16)

    down_grad = grads(far(grad_mixed), mine_and_far(hidden)).reshape(width, 2, -1)
    up_grad = grads(far(normed_low), mine_and_far(grad_pre)).reshape(width, 2, -1)
    down_total = scatter_sum(down_grad, dp_count)
    up_total = scatter_sum(up_grad, dp_count)

    grad_normed = grad_two + dot(grad_pre[0], w_up[0], 1, 1) + dot(grad_pre[1], w_up[1], 1, 1)
    grad_one, attn_gain_term, attn_shift_term = norm_backward(grad_normed, unit_one, inverse_one, attn_gain)
    grad_attended = grad_one.astype(bf16)
    out_bias_term = jnp.sum(grad_one, axis=0)
    grad_attended, down_grad, up_grad = lax.optimization_barrier((grad_attended, down_grad, up_grad))
    grad_context = [dot(grad_attended, w_out[r], 1, 0).astype(bf16) for r in range(2)]
    back = [attend_back(qkv[r], probs[r], grad_context[r]) for r in range(2)]
    grad_qkv = [b[0] for b in back]
    sums = jnp.stack([b[1] for b in back])[:, :, :, 0]
    sent_back = dot(grad_qkv[0], w_qkv[0], 1, 1) + dot(grad_qkv[1], w_qkv[1], 1, 1)
    input_grad = (grad_one + sent_back).astype(bf16)

    qkv_grad = grads(jnp.concatenate([flat, flat_far], 0), mine_and_far(grad_qkv)).reshape(width, 2, -1)
    out_grad = grads(far(grad_attended), mine_and_far(context)).reshape(width, 2, -1)
    one_total = scatter_sum(jnp.concatenate([qkv_grad, out_grad], 2), dp_count)

    def settle(values):
        values = jnp.where(c == 0, values, values[::-1])
        values = jnp.where(t == 0, values, values[:, ::-1])
        return values.transpose(1, 0, 2).reshape(-1)

    small = jnp.concatenate(
        [settle(sums[:, :, 0]), settle(sums[:, :, 1]), settle(up_bias_term.reshape(2, 2, -1)), out_bias_term, down_bias_term, attn_gain_term, attn_shift_term, mlp_gain_term, mlp_shift_term]
    )
    small = lax.all_gather(small.reshape(-1, 128), ("dp", "ctx", "tp"), axis=0, tiled=False)
    small = jnp.sum(small, axis=0).reshape(-1)

    def cut_tp(start, size):
        return lax.dynamic_slice_in_dim(small, start + t * (size // 2), size // 2)

    at = 2 * inner + ff
    vectors = [lax.slice_in_dim(small, at + i * width, at + (i + 1) * width) for i in range(6)]

    def spread(values):
        got = swap(values[half:], "ctx")
        pair = order(c, values[None, :half], got[None], 0)
        return order(t, pair, swap(pair, "tp"), 0)

    totals = jnp.stack([one_total, up_total, down_total])
    totals = totals.reshape(3, 2, piece_rows, unit)
    shards = order(c, take(totals, c, 1)[None], swap(take(totals, 1 - c, 1), "ctx")[None], 0)
    one_shard = shards[:, 0].reshape(2, piece_rows, 4, -1).transpose(2, 1, 0, 3).reshape(4, piece_rows, -1)
    up_shard = shards[:, 1].transpose(1, 0, 2).reshape(piece_rows, -1)
    down_shard = shards[:, 2].transpose(1, 0, 2).reshape(piece_rows, -1).T
    return (
        spread(output.astype(bf16)),
        spread(input_grad),
        one_shard[0],
        one_shard[1],
        one_shard[2],
        one_shard[3].T,
        up_shard,
        down_shard,
        cut_tp(0, inner),
        cut_tp(inner, inner),
        vectors[0],
        cut_tp(2 * inner, ff),
        *vectors[1:],
    )


def solution(mesh):
    weight_in, weight_out = P(("dp", "ctx"), "tp"), P("tp", ("dp", "ctx"))
    rows = P("dp", "ctx", None)
    weights = (weight_in, weight_in, weight_in, weight_out, weight_in, weight_out)
    vectors = (P("tp"), P("tp"), P(), P("tp"), P(), P(), P(), P(), P())
    dp_count = mesh.shape["dp"]

    def run(*args):
        return body(dp_count, *args)

    return jax.shard_map(
        run,
        mesh=mesh,
        in_specs=(rows, P("dp", None), *weights, *vectors, rows),
        out_specs=(rows, rows, *weights, *vectors),
        check_vma=False,
    )
```

time: 724 us -> 909 us (1.26)
  Pallas kernels: 0 us -> 415 us
  local copies, waits for them, and re-layouts: 183 us -> 67.9 us
  waiting for transfers between devices: 236 us -> 165 us
  starting transfers between devices: 37 us -> 101 us
  blocking collectives: 53.7 us -> 0 us
  matrix products: 115 us -> 85.9 us
  other arithmetic: 71.1 us -> 50.6 us
    pallas_call x0 -> x7, Pallas kernels: none -> 415 us  [the longest x3 387 us: gather_weights(): pl.pallas_call(functools.partial(assemble_kernel, cuts), out_shape=[jax.S...]
    all_gather x3 -> x1, waiting for transfers between devices: 154 us -> 0.01 us  [body(): lax.all_gather(small.reshape(-1, 128), ('dp', 'ctx', 'tp'), axis=0, tiled...]
    ppermute x15 -> x30, starting transfers between devices: 25.2 us -> 82.2 us  [the longest x18 69.3 us: shift_z(): lax.ppermute(values, 'dp', [(i, (i + 2 * step) % 8) for i in range(8)])]
    ppermute x24 -> x31, waiting for transfers between devices: 43.9 us -> 86.2 us  [swap(): return lax.ppermute(values, axis, [(0, 1), (1, 0)])]
    ppermute x15 -> x30, waiting for transfers between devices: 37.9 us -> 79.1 us  [the longest x18 45.6 us: shift_z(): lax.ppermute(values, 'dp', [(i, (i + 2 * step) % 8) for i in range(8)])]
    psum x1 -> x0, blocking collectives: 39.8 us -> none  [body(): small = lax.psum(small.reshape(-1, 128), ('dp', 'ctx', 'tp')).reshape(-1)]
    dynamic_slice x17 -> x5, local copies, waits for them, and re-layouts: 46.3 us -> 10.3 us  [take(): return lax.dynamic_index_in_dim(values, index, axis, keepdims=False)]
    unnamed x168 -> x132, local copies, waits for them, and re-layouts: 46.4 us -> 11.7 us
  transfers between devices with their start and end apart: 42 -> 62, of which waited for: 14 -> 17; matrix products, arithmetic and copies ran while one was open for 49% -> 16% of each run, Pallas kernels for 0% -> 46%
where the time goes in v2:
time: 909 us; the launch traced here: 902 us
  Pallas kernels  415 us (46%)
  waiting for transfers between devices  165 us (18%)
  starting transfers between devices  101 us (11%)
  matrix products  85.9 us (9%)
  local copies, waits for them, and re-layouts  67.9 us (7%)
  other arithmetic  50.6 us (6%)
  between operations  15.9 us (2%)
    pallas_call x3, Pallas kernels, gather_weights(): pl.pallas_call(functools.partial(assemble_kernel, cuts), out_shape=[jax.S...  387 us
    ppermute x31, waiting for transfers between devices, swap(): return lax.ppermute(values, axis, [(0, 1), (1, 0)])  86.2 us
    dot_general x20, matrix products, dot(): lax.dot_general(left, right, (((left_dim,), (right_dim,)), ((), ())), pre...  85.9 us
    ppermute x18, starting transfers between devices, shift_z(): lax.ppermute(values, 'dp', [(i, (i + 2 * step) % 8) for i in range(8)])  69.3 us
    ppermute x18, waiting for transfers between devices, shift_z(): lax.ppermute(values, 'dp', [(i, (i + 2 * step) % 8) for i in range(8)])  45.6 us
    ppermute x12, waiting for transfers between devices, swap_x(): return lax.ppermute(values, 'dp', [(i, i ^ 1) for i in range(8)])  33.5 us
    ppermute x31, starting transfers between devices, swap(): return lax.ppermute(values, axis, [(0, 1), (1, 0)])  19.1 us
  transfers between devices with their start and end apart: 62, of which 17 were waited for; matrix products, arithmetic and copies ran while one was open for 16% of the time, Pallas kernels for 46%

profile of v2, /device:TPU:0, one launch (start us, length us, event | category | flops | bytes accessed | tf_op | source)
XLA Modules:
  0.0 902.4 jit_solution(13333072693706714206)
XLA Ops:
  33.1 6.4 collective-permute-done.5
  39.4 5.2 collective-permute-start.12
  44.6 10.8 %collective-permute-start.22 = (bf16[128,1024]{1,0:T(8,128)(2,1)}, bf16[128,1024]{1,0:T(8,128)(2,1)S(1)}, u32[]{:S(2)}, u32[]{:S(2)}) collective-permute-start(bf16[128,1024]{1,0:T(8,128)(2,1)} %get-tuple-element.95), channel_id=1, source_target_pairs={{0,16},{4,20},{8,24},{12,28},{16,0},{20,4},{24,8},{28,12},{1,17},{... | collective-permute-start | bytes 786440 | tf_op jit(solution)/shard_map/ppermute | solution.py:47
  55.7 16.4 %collective-permute-done.15 = bf16[128,1024]{1,0:T(8,128)(2,1)S(1)} collective-permute-done((bf16[128,1024]{1,0:T(8,128)(2,1)S(1)}, bf16[128,1024]{1,0:T(8,128)(2,1)S(1)}, u32[]{:S(2)}, u32[]{:S(2)}) %collective-permute-start.15) | collective-permute-done | bytes 262176 | tf_op jit(solution)/shard_map/ppermute | solution.py:47
  76.4 7.0 collective-permute-done.22
  83.3 5.3 collective-permute-start.19
  91.6 6.5 collective-permute-done.19
  106.9 29.1 %collective-permute-done.24 = bf16[2,128,1024]{2,1,0:T(8,128)(2,1)S(1)} collective-permute-done((bf16[2,128,1024]{2,1,0:T(8,128)(2,1)S(1)}, bf16[2,128,1024]{2,1,0:T(8,128)(2,1)S(1)}, u32[]{:S(2)}, u32[]{:S(2)}) %collective-permute-start.24) | collective-permute-done | bytes 524320 | tf_op jit(solution)/shard_map/ppermute | solution.py:39
  141.0 128.8 %assemble.3 = (bf16[1024,1536]{1,0:T(8,128)(2,1)}, bf16[1024,512]{1,0:T(8,128)(2,1)}) custom-call(s32[2]{0:T(128)} %pad_add_fusion.1.place, bf16[2,2,128,1024]{3,2,1,0:T(8,128)(2,1)} %copy-done.20, bf16[2,2,128,1024]{3,2,1,0:T(8,128)(2,1)} %copy-done.32, bf16[2,2,128,1024]{3,2,1,0:T(8,128)(2,1)} %copy-done.19, bf16[2,2,128,1024]{3,2,1,0:T(8,128)(2,1)} %copy-done.31), custom_call_target="tpu_custom_call" | custom-call | tf_op jit(solution)/shard_map/assemble/pallas_call | solution.py:103
  276.6 21.4 %collective-permute-done.21.one_y = bf16[2,2,128,1024]{3,2,1,0:T(8,128)(2,1)} collective-permute-done((bf16[2,2,128,1024]{3,2,1,0:T(8,128)(2,1)}, bf16[2,2,128,1024]{3,2,1,0:T(8,128)(2,1)}, u32[]{:S(2)}, u32[]{:S(2)}) %collective-permute-start.21) | collective-permute-done | bytes 1048608 | tf_op jit(solution)/shard_map/ppermute | solution.py:39
  298.0 128.8 %assemble.5 = bf16[1024,2048]{1,0:T(8,128)(2,1)} custom-call(s32[2]{0:T(128)} %pad_add_fusion.1.place, bf16[2,2,128,1024]{3,2,1,0:T(8,128)(2,1)} %pad_maximum_fusion.8.one, bf16[2,2,128,1024]{3,2,1,0:T(8,128)(2,1)} %collective-permute-done.21.one_y, bf16[2,2,128,1024]{3,2,1,0:T(8,128)(2,1)} %pad_maximum_fusion.9.two, ...), custom_call_target="tpu_custom_call" | custom-call | tf_op jit(solution)/shard_map/assemble/pallas_call | solution.py:103
  426.9 128.8 %assemble.4 = bf16[1024,2048]{1,0:T(8,128)(2,1)} custom-call(s32[2]{0:T(128)} %pad_add_fusion.1.place, bf16[2,2,128,1024]{3,2,1,0:T(8,128)(2,1)} %copy-done.18, bf16[2,2,128,1024]{3,2,1,0:T(8,128)(2,1)} %collective-permute-done.14.one_y, bf16[2,2,128,1024]{3,2,1,0:T(8,128)(2,1)} %copy-done.17, bf16[2,2,128,1024]{3,2,1,0:T(8,128)(2,1)} %collective-permute-done.18.two_x), custom_call_target="tpu_custom_call" | custom-call | tf_op jit(solution)/shard_map/assemble/pallas_call | solution.py:103
  560.2 6.8 attend.2
  572.8 6.8 attend.3
  588.4 5.9 multiply_convert_fusion.2
  594.4 6.7 fusion.137
  611.0 5.0 convert_reduce_fusion.1
  618.4 7.0 convert_reduce_fusion
  625.4 4.9 multiply_reduce_fusion
  635.4 7.6 attend_back.2
  645.9 7.6 attend_back.3
  676.9 5.5 convolution_convert_fusion
  689.4 6.8 fusion.21
  698.6 6.8 fusion.18
  715.6 5.5 constant_dynamic-slice_fusion.3
  747.4 33.5 %collective-permute-done.36 = bf16[2,128,1024]{2,1,0:T(8,128)(2,1)S(1)} collective-permute-done((bf16[2,128,1024]{2,1,0:T(8,128)(2,1)S(1)}, bf16[2,128,1024]{2,1,0:T(8,128)(2,1)S(1)}, u32[]{:S(2)}, u32[]{:S(2)}) %collective-permute-start.36) | collective-permute-done | bytes 524320 | tf_op jit(solution)/shard_map/ppermute | solution.py:43
  795.4 11.6 %collective-permute-done.53 = bf16[2,2,128,1024]{3,2,0,1:T(8,128)(2,1)S(1)} collective-permute-done((bf16[2,2,128,1024]{3,2,0,1:T(8,128)(2,1)S(1)}, bf16[2,2,128,1024]{3,2,0,1:T(8,128)(2,1)S(1)}, u32[]{:S(2)}, u32[]{:S(2)}) %collective-permute-start.53) | collective-permute-done | bytes 1048608 | tf_op jit(solution)/shard_map/ppermute | solution.py:39
  808.5 7.4 collective-permute-done.47
  818.5 9.1 %collective-permute-done.56 = bf16[2,128,1024]{2,1,0:T(8,128)(2,1)S(1)} collective-permute-done((bf16[2,128,1024]{2,1,0:T(8,128)(2,1)S(1)}, bf16[2,128,1024]{2,1,0:T(8,128)(2,1)S(1)}, u32[]{:S(2)}, u32[]{:S(2)}) %collective-permute-start.56) | collective-permute-done | bytes 524320 | tf_op jit(solution)/shard_map/ppermute | solution.py:39
  838.7 8.8 collective-permute-start.57
  849.4 15.1 %collective-permute-start.59 = (bf16[128,1024]{1,0:T(8,128)(2,1)S(1)}, bf16[128,1024]{1,0:T(8,128)(2,1)S(1)}, u32[]{:S(2)}, u32[]{:S(2)}) collective-permute-start(bf16[128,1024]{1,0:T(8,128)(2,1)S(1)} %get-tuple-element.87), channel_id=1, source_target_pairs={{0,24},{4,28},{8,0},{12,4},{16,8},{20,12},{24,16},{28,20},{1,25},{... | collective-permute-start | bytes 786440 | tf_op jit(solution)/shard_map/ppermute | solution.py:47
  865.6 5.3 collective-permute-done.59
  (400 shorter events, 218.1 us)
Async XLA Ops:
  7.2 874.1 %all-gather.2.cloned.1.call-start = ((), (), s32[]{:S(2)}) async-start(), calls=%async_computation | async-start | bytes 1622016 | tf_op jit(solution)/shard_map/all_gather | solution.py:346
  29.1 43.1 %collective-permute-start.15 = (bf16[128,1024]{1,0:T(8,128)(2,1)S(1)}, bf16[128,1024]{1,0:T(8,128)(2,1)S(1)}, u32[]{:S(2)}, u32[]{:S(2)}) collective-permute-start(bf16[128,1024]{1,0:T(8,128)(2,1)S(1)} %get-tuple-element.94), channel_id=1, source_target_pairs={{0,16},{4,20},{8,24},{12,28},{16,0},{20,4},{24,8},{28,12},{1,17},{... | collective-permute-start | bytes 786440 | tf_op jit(solution)/shard_map/ppermute | solution.py:47
  30.1 43.5 %collective-permute-start.16 = (bf16[128,1024]{1,0:T(8,128)(2,1)S(1)}, bf16[128,1024]{1,0:T(8,128)(2,1)S(1)}, u32[]{:S(2)}, u32[]{:S(2)}) collective-permute-start(bf16[128,1024]{1,0:T(8,128)(2,1)S(1)} %get-tuple-element.94), channel_id=1, source_target_pairs={{0,24},{4,28},{8,0},{12,4},{16,8},{20,12},{24,16},{28,20},{1,25},{... | collective-permute-start | bytes 786440 | tf_op jit(solution)/shard_map/ppermute | solution.py:47
  39.4 34.3 %collective-permute-start.12 = (bf16[128,1024]{1,0:T(8,128)(2,1)S(1)}, bf16[128,1024]{1,0:T(8,128)(2,1)S(1)}, u32[]{:S(2)}, u32[]{:S(2)}) collective-permute-start(bf16[128,1024]{1,0:T(8,128)(2,1)S(1)} %get-tuple-element.94), channel_id=1, source_target_pairs={{0,8},{4,12},{8,16},{12,20},{16,24},{20,28},{24,0},{28,4},{1,9},{5... | collective-permute-start | bytes 786440 | tf_op jit(solution)/shard_map/ppermute | solution.py:47
  44.6 38.7 %collective-permute-start.22 = (bf16[128,1024]{1,0:T(8,128)(2,1)}, bf16[128,1024]{1,0:T(8,128)(2,1)S(1)}, u32[]{:S(2)}, u32[]{:S(2)}) collective-permute-start(bf16[128,1024]{1,0:T(8,128)(2,1)} %get-tuple-element.95), channel_id=1, source_target_pairs={{0,16},{4,20},{8,24},{12,28},{16,0},{20,4},{24,8},{28,12},{1,17},{... | collective-permute-start | bytes 786440 | tf_op jit(solution)/shard_map/ppermute | solution.py:47
  55.5 33.2 %collective-permute-start.7 = (bf16[2,128,1024]{2,1,0:T(8,128)(2,1)S(1)}, bf16[2,128,1024]{2,1,0:T(8,128)(2,1)S(1)}, u32[]{:S(2)}, u32[]{:S(2)}) collective-permute-start(bf16[2,128,1024]{2,1,0:T(8,128)(2,1)S(1)} %get-tuple-element.113), channel_id=1, source_target_pairs={{0,1},{1,0},{2,3},{3,2},{4,5},{5,4},{6,7},{7,6},{8,9},{9,8},{10,11... | collective-permute-start | bytes 1572872 | tf_op jit(solution)/shard_map/ppermute | solution.py:39
  73.6 198.5 %collective-permute-start = (bf16[3,256,1024]{2,1,0:T(8,128)(2,1)}, bf16[3,256,1024]{2,1,0:T(8,128)(2,1)}, u32[]{:S(2)}, u32[]{:S(2)}) collective-permute-start(bf16[3,256,1024]{2,1,0:T(8,128)(2,1)} %pad_maximum_fusion.1), channel_id=1, source_target_pairs={{0,2},{2,0},{1,3},{3,1},{4,6},{6,4},{5,7},{7,5},{8,10},{10,8},{9,1... | collective-permute-start | bytes 4718600 | tf_op jit(solution)/shard_map/ppermute | solution.py:39
  91.0 47.5 %collective-permute-start.8 = (bf16[2,2,128,1024]{3,2,1,0:T(8,128)(2,1)S(1)}, bf16[2,2,128,1024]{3,2,1,0:T(8,128)(2,1)S(1)}, u32[]{:S(2)}, u32[]{:S(2)}) collective-permute-start(bf16[2,2,128,1024]{3,2,1,0:T(8,128)(2,1)S(1)} %pad_maximum_fusion.5.two), channel_id=1, source_target_pairs={{0,4},{4,0},{8,12},{12,8},{16,20},{20,16},{24,28},{28,24},{1,5},{5... | collective-permute-start | bytes 3145736 | tf_op jit(solution)/shard_map/ppermute | solution.py:43
  98.1 41.0 %collective-permute-start.4 = (bf16[2,2,128,1024]{3,2,1,0:T(8,128)(2,1)S(1)}, bf16[2,2,128,1024]{3,2,1,0:T(8,128)(2,1)S(1)}, u32[]{:S(2)}, u32[]{:S(2)}) collective-permute-start(bf16[2,2,128,1024]{3,2,1,0:T(8,128)(2,1)S(1)} %pad_maximum_fusion.4.one), channel_id=1, source_target_pairs={{0,1},{1,0},{2,3},{3,2},{4,5},{5,4},{6,7},{7,6},{8,9},{9,8},{10,11... | collective-permute-start | bytes 3145736 | tf_op jit(solution)/shard_map/ppermute | solution.py:39
  103.5 32.4 %collective-permute-start.24 = (bf16[2,128,1024]{2,1,0:T(8,128)(2,1)S(1)}, bf16[2,128,1024]{2,1,0:T(8,128)(2,1)S(1)}, u32[]{:S(2)}, u32[]{:S(2)}) collective-permute-start(bf16[2,128,1024]{2,1,0:T(8,128)(2,1)S(1)} %get-tuple-element.105), channel_id=1, source_target_pairs={{0,1},{1,0},{2,3},{3,2},{4,5},{5,4},{6,7},{7,6},{8,9},{9,8},{10,11... | collective-permute-start | bytes 1572872 | tf_op jit(solution)/shard_map/ppermute | solution.py:39
  105.1 164.8 %collective-permute-start.20 = (bf16[2,128,1024]{2,1,0:T(8,128)(2,1)}, bf16[2,128,1024]{2,1,0:T(8,128)(2,1)}, u32[]{:S(2)}, u32[]{:S(2)}) collective-permute-start(bf16[2,128,1024]{2,1,0:T(8,128)(2,1)} %get-tuple-element.107), channel_id=1, source_target_pairs={{0,4},{4,0},{8,12},{12,8},{16,20},{20,16},{24,28},{28,24},{1,5},{5... | collective-permute-start | bytes 1572872 | tf_op jit(solution)/shard_map/ppermute | solution.py:43
  136.0 290.9 %collective-permute-start.18 = (bf16[2,2,128,1024]{3,2,1,0:T(8,128)(2,1)S(1)}, bf16[2,2,128,1024]{3,2,1,0:T(8,128)(2,1)}, u32[]{:S(2)}, u32[]{:S(2)}) collective-permute-start(bf16[2,2,128,1024]{3,2,1,0:T(8,128)(2,1)S(1)} %pad_maximum_fusion.7.two), channel_id=1, source_target_pairs={{0,4},{4,0},{8,12},{12,8},{16,20},{20,16},{24,28},{28,24},{1,5},{5... | collective-permute-start | bytes 3145736 | tf_op jit(solution)/shard_map/ppermute | solution.py:43
  138.5 288.4 %collective-permute-start.14 = (bf16[2,2,128,1024]{3,2,1,0:T(8,128)(2,1)S(1)}, bf16[2,2,128,1024]{3,2,1,0:T(8,128)(2,1)}, u32[]{:S(2)}, u32[]{:S(2)}) collective-permute-start(bf16[2,2,128,1024]{3,2,1,0:T(8,128)(2,1)S(1)} %pad_maximum_fusion.6.one), channel_id=1, source_target_pairs={{0,1},{1,0},{2,3},{3,2},{4,5},{5,4},{6,7},{7,6},{8,9},{9,8},{10,11... | collective-permute-start | bytes 3145736 | tf_op jit(solution)/shard_map/ppermute | solution.py:39
  140.5 135.8 %collective-permute-start.25 = (bf16[2,2,128,1024]{3,2,1,0:T(8,128)(2,1)}, bf16[2,2,128,1024]{3,2,1,0:T(8,128)(2,1)}, u32[]{:S(2)}, u32[]{:S(2)}) collective-permute-start(bf16[2,2,128,1024]{3,2,1,0:T(8,128)(2,1)} %pad_maximum_fusion.9.two), channel_id=1, source_target_pairs={{0,4},{4,0},{8,12},{12,8},{16,20},{20,16},{24,28},{28,24},{1,5},{5... | collective-permute-start | bytes 3145736 | tf_op jit(solution)/shard_map/ppermute | solution.py:43
  269.9 299.1 %collective-permute-start.10 = (bf16[1024,1536]{1,0:T(8,128)(2,1)}, bf16[1024,1536]{1,0:T(8,128)(2,1)}, u32[]{:S(2)}, u32[]{:S(2)}) collective-permute-start(bf16[1024,1536]{1,0:T(8,128)(2,1)} %get-tuple-element.27), channel_id=1, source_target_pairs={{0,2},{2,0},{1,3},{3,1},{4,6},{6,4},{5,7},{7,5},{8,10},{10,8},{9,1... | collective-permute-start | bytes 9437192 | tf_op jit(solution)/shard_map/ppermute | solution.py:39
  276.3 303.2 %collective-permute-start.11 = (bf16[1024,512]{1,0:T(8,128)(2,1)}, bf16[1024,512]{1,0:T(8,128)(2,1)}, u32[]{:S(2)}, u32[]{:S(2)}) collective-permute-start(bf16[1024,512]{1,0:T(8,128)(2,1)} %get-tuple-element.29), channel_id=1, source_target_pairs={{0,2},{2,0},{1,3},{3,1},{4,6},{6,4},{5,7},{7,5},{8,10},{10,8},{9,1... | collective-permute-start | bytes 3145736 | tf_op jit(solution)/shard_map/ppermute | solution.py:39
  426.8 167.5 %collective-permute-start.27 = (bf16[1024,2048]{1,0:T(8,128)(2,1)}, bf16[1024,2048]{1,0:T(8,128)(2,1)}, u32[]{:S(2)}, u32[]{:S(2)}) collective-permute-start(bf16[1024,2048]{1,0:T(8,128)(2,1)} %assemble.5), channel_id=1, source_target_pairs={{0,2},{2,0},{1,3},{3,1},{4,6},{6,4},{5,7},{7,5},{8,10},{10,8},{9,1... | collective-permute-start | bytes 12582920 | tf_op jit(solution)/shard_map/ppermute | solution.py:39
  555.8 32.7 %collective-permute-start.26 = (bf16[1024,2048]{1,0:T(8,128)(2,1)}, bf16[1024,2048]{1,0:T(8,128)(2,1)S(1)}, u32[]{:S(2)}, u32[]{:S(2)}) collective-permute-start(bf16[1024,2048]{1,0:T(8,128)(2,1)} %assemble.4), channel_id=1, source_target_pairs={{0,2},{2,0},{1,3},{3,1},{4,6},{6,4},{5,7},{7,5},{8,10},{10,8},{9,1... | collective-permute-start | bytes 12582920 | tf_op jit(solution)/shard_map/ppermute | solution.py:39
  634.5 35.6 %collective-permute-start.33 = (bf16[512,1024]{1,0:T(8,128)(2,1)}, bf16[512,1024]{1,0:T(8,128)(2,1)}, u32[]{:S(2)}, u32[]{:S(2)}) collective-permute-start(bf16[512,1024]{1,0:T(8,128)(2,1)} %convert_element_type.280), channel_id=1, source_target_pairs={{0,2},{2,0},{1,3},{3,1},{4,6},{6,4},{5,7},{7,5},{8,10},{10,8},{9,1... | collective-permute-start | bytes 3145736 | tf_op jit(solution)/shard_map/ppermute | solution.py:39
  634.6 54.8 %collective-permute-start.43 = (bf16[512,2048]{1,0:T(8,128)(2,1)}, bf16[512,2048]{1,0:T(8,128)(2,1)}, u32[]{:S(2)}, u32[]{:S(2)}) collective-permute-start(bf16[512,2048]{1,0:T(8,128)(2,1)} %get-tuple-element.143), channel_id=1, source_target_pairs={{0,2},{2,0},{1,3},{3,1},{4,6},{6,4},{5,7},{7,5},{8,10},{10,8},{9,1... | collective-permute-start | bytes 6291464 | tf_op jit(solution)/shard_map/ppermute | solution.py:39
  685.7 52.7 %collective-permute-start.37 = (bf16[2,128,2,1024]{3,1,0,2:T(8,128)(2,1)}, bf16[2,128,2,1024]{3,1,0,2:T(8,128)(2,1)}, u32[]{:S(2)}, u32[]{:S(2)}) collective-permute-start(bf16[2,128,2,1024]{3,1,0,2:T(8,128)(2,1)} %dynamic-slice_bitcast_fusion), channel_id=1, source_target_pairs={{0,4},{4,0},{8,12},{12,8},{16,20},{20,16},{24,28},{28,24},{1,5},{5... | collective-permute-start | bytes 3145736 | tf_op jit(solution)/shard_map/ppermute | solution.py:43
  688.3 53.4 %collective-permute-start.35 = (bf16[2,2,128,1024]{3,2,1,0:T(8,128)(2,1)}, bf16[2,2,128,1024]{3,2,1,0:T(8,128)(2,1)}, u32[]{:S(2)}, u32[]{:S(2)}) collective-permute-start(bf16[2,2,128,1024]{3,2,1,0:T(8,128)(2,1)} %slice_bitcast_fusion), channel_id=1, source_target_pairs={{0,1},{1,0},{2,3},{3,2},{4,5},{5,4},{6,7},{7,6},{8,9},{9,8},{10,11... | collective-permute-start | bytes 3145736 | tf_op jit(solution)/shard_map/ppermute | solution.py:39
  722.3 65.8 %collective-permute-start.46 = (bf16[2,128,2,1024]{3,1,0,2:T(8,128)(2,1)}, bf16[2,128,2,1024]{3,1,0,2:T(8,128)(2,1)}, u32[]{:S(2)}, u32[]{:S(2)}) collective-permute-start(bf16[2,128,2,1024]{3,1,0,2:T(8,128)(2,1)} %bitcast.322), channel_id=1, source_target_pairs={{0,4},{4,0},{8,12},{12,8},{16,20},{20,16},{24,28},{28,24},{1,5},{5... | collective-permute-start | bytes 3145736 | tf_op jit(solution)/shard_map/ppermute | solution.py:43
  731.5 51.4 %collective-permute-start.44 = (bf16[2,2,128,1024]{3,2,0,1:T(8,128)(2,1)}, bf16[2,2,128,1024]{3,2,0,1:T(8,128)(2,1)}, u32[]{:S(2)}, u32[]{:S(2)}) collective-permute-start(bf16[2,2,128,1024]{3,2,0,1:T(8,128)(2,1)} %bitcast.320), channel_id=1, source_target_pairs={{0,1},{1,0},{2,3},{3,2},{4,5},{5,4},{6,7},{7,6},{8,9},{9,8},{10,11... | collective-permute-start | bytes 3145736 | tf_op jit(solution)/shard_map/ppermute | solution.py:39
  733.6 59.0 %collective-permute-start.55 = (bf16[2,128,2,1024]{3,1,0,2:T(8,128)(2,1)}, bf16[2,128,2,1024]{3,1,0,2:T(8,128)(2,1)}, u32[]{:S(2)}, u32[]{:S(2)}) collective-permute-start(bf16[2,128,2,1024]{3,1,0,2:T(8,128)(2,1)} %bitcast.321), channel_id=1, source_target_pairs={{0,4},{4,0},{8,12},{12,8},{16,20},{20,16},{24,28},{28,24},{1,5},{5... | collective-permute-start | bytes 3145736 | tf_op jit(solution)/shard_map/ppermute | solution.py:43
  740.5 41.6 %collective-permute-start.38 = (bf16[2,128,1024]{2,1,0:T(8,128)(2,1)S(1)}, bf16[2,128,1024]{2,1,0:T(8,128)(2,1)S(1)}, u32[]{:S(2)}, u32[]{:S(2)}) collective-permute-start(bf16[2,128,1024]{2,1,0:T(8,128)(2,1)S(1)} %slice_bitcast_fusion.6), channel_id=1, source_target_pairs={{0,1},{1,0},{2,3},{3,2},{4,5},{5,4},{6,7},{7,6},{8,9},{9,8},{10,11... | collective-permute-start | bytes 1572872 | tf_op jit(solution)/shard_map/ppermute | solution.py:39
  743.4 37.5 %collective-permute-start.36 = (bf16[2,128,1024]{2,1,0:T(8,128)(2,1)S(1)}, bf16[2,128,1024]{2,1,0:T(8,128)(2,1)S(1)}, u32[]{:S(2)}, u32[]{:S(2)}) collective-permute-start(bf16[2,128,1024]{2,1,0:T(8,128)(2,1)S(1)} %dynamic-slice_bitcast_fusion.4), channel_id=1, source_target_pairs={{0,4},{4,0},{8,12},{12,8},{16,20},{20,16},{24,28},{28,24},{1,5},{5... | collective-permute-start | bytes 1572872 | tf_op jit(solution)/shard_map/ppermute | solution.py:43
  782.6 45.2 %collective-permute-start.39 = (bf16[128,1024]{1,0:T(8,128)(2,1)S(1)}, bf16[128,1024]{1,0:T(8,128)(2,1)S(1)}, u32[]{:S(2)}, u32[]{:S(2)}) collective-permute-start(bf16[128,1024]{1,0:T(8,128)(2,1)S(1)} %get-tuple-element.79), channel_id=1, source_target_pairs={{0,8},{4,12},{8,16},{12,20},{16,24},{20,28},{24,0},{28,4},{1,9},{5... | collective-permute-start | bytes 786440 | tf_op jit(solution)/shard_map/ppermute | solution.py:47
  782.9 51.5 %collective-permute-start.40 = (bf16[128,1024]{1,0:T(8,128)(2,1)S(1)}, bf16[128,1024]{1,0:T(8,128)(2,1)S(1)}, u32[]{:S(2)}, u32[]{:S(2)}) collective-permute-start(bf16[128,1024]{1,0:T(8,128)(2,1)S(1)} %get-tuple-element.80), channel_id=1, source_target_pairs={{0,16},{4,20},{8,24},{12,28},{16,0},{20,4},{24,8},{28,12},{1,17},{... | collective-permute-start | bytes 786440 | tf_op jit(solution)/shard_map/ppermute | solution.py:47
  788.1 47.5 %collective-permute-start.41 = (bf16[128,1024]{1,0:T(8,128)(2,1)S(1)}, bf16[128,1024]{1,0:T(8,128)(2,1)S(1)}, u32[]{:S(2)}, u32[]{:S(2)}) collective-permute-start(bf16[128,1024]{1,0:T(8,128)(2,1)S(1)} %get-tuple-element.81), channel_id=1, source_target_pairs={{0,24},{4,28},{8,0},{12,4},{16,8},{20,12},{24,16},{28,20},{1,25},{... | collective-permute-start | bytes 786440 | tf_op jit(solution)/shard_map/ppermute | solution.py:47
  834.4 37.9 %collective-permute-start.31 = (bf16[2,256,1024]{2,1,0:T(8,128)(2,1)S(1)}, bf16[2,256,1024]{2,1,0:T(8,128)(2,1)}, u32[]{:S(2)}, u32[]{:S(2)}) collective-permute-start(bf16[2,256,1024]{2,1,0:T(8,128)(2,1)S(1)} %copy-done.15), channel_id=1, source_target_pairs={{0,1},{1,0},{2,3},{3,2},{4,5},{5,4},{6,7},{7,6},{8,9},{9,8},{10,11... | collective-permute-start | bytes 3145736 | tf_op jit(solution)/shard_map/ppermute | solution.py:39
  835.5 42.6 %collective-permute-start.29 = (bf16[2,256,1024]{2,1,0:T(8,128)(2,1)S(1)}, bf16[2,256,1024]{2,1,0:T(8,128)(2,1)}, u32[]{:S(2)}, u32[]{:S(2)}) collective-permute-start(bf16[2,256,1024]{2,1,0:T(8,128)(2,1)S(1)} %copy-done.16), channel_id=1, source_target_pairs={{0,1},{1,0},{2,3},{3,2},{4,5},{5,4},{6,7},{7,6},{8,9},{9,8},{10,11... | collective-permute-start | bytes 3145736 | tf_op jit(solution)/shard_map/ppermute | solution.py:39
  (84 other events, 1631.4 us)
Sparse Core Ops, SparseCore 0:
  664.5 58.6 all-gather.1

commit v3 on v2

--- a/solution.py
+++ b/solution.py
@@ -63,6 +63,7 @@
     outs, sems = rest[: len(cuts)], rest[len(cuts)]
     z, x = place[0], place[1]
     rows = one.shape[2]
+    copies = []
     for k in range(4):
         for far_x in range(2):
             block = lax.rem(z + 4 - k, 4) * 2 + lax.rem(x + far_x, 2)
@@ -73,13 +74,16 @@
                 else:
                     source = (two_x if far_x else two).at[far_t, k - 2]
                 for n, (start, size) in enumerate(cuts):
-                    pltpu.make_async_copy(
-                        source.at[:, start : start + size],
-                        outs[n].at[at, far_t * size : far_t * size + size],
-                        sems.at[n],
-                    ).start()
-    for n in range(len(cuts)):
-        pltpu.make_async_copy(outs[n], outs[n], sems.at[n]).wait()
+                    copies.append(
+                        pltpu.make_async_copy(
+                            source.at[:, start : start + size],
+                            outs[n].at[at, far_t * size : far_t * size + size],
+                            sems.at[len(copies)],
+                        )
+                    )
+                    copies[-1].start()
+    for copy in copies:
+        copy.wait()
 
 
 def gather_weights(piece, cuts, place, dp_count):
@@ -104,8 +108,9 @@
         functools.partial(assemble_kernel, cuts),
         out_shape=[jax.ShapeDtypeStruct((total, 2 * n), bf16) for _, n in cuts],
         in_specs=[pl.BlockSpec(memory_space=pltpu.SMEM)] + [anyspace] * 4,
-        out_specs=[anyspace] * len(cuts),
-        scratch_shapes=[pltpu.SemaphoreType.DMA((len(cuts),))],
+        out_specs=[pl.BlockSpec(memory_space=pltpu.VMEM)] * len(cuts),
+        scratch_shapes=[pltpu.SemaphoreType.DMA((16 * len(cuts),))],
+        compiler_params=pltpu.CompilerParams(vmem_limit_bytes=24 << 20),
         name="assemble",
     )(place, one, one_y, two, two_x)
 
@@ -156,7 +161,8 @@
     )(qkv, seg.reshape(rows, 1), seg.reshape(1, rows))
 
 
-def attend_back_kernel(qkv, probs, upstream, grads, sums):
+def attend_back_kernel(qkv, probs, upstream, *rest):
+    grads, sums = rest[-2:]
     quarter = qkv.shape[1] // 3
     low = lax.broadcasted_iota(jnp.int32, (1, LANES), 1) < HEAD_DIM
     for pair in range(quarter // LANES):
@@ -186,7 +192,7 @@
             sums[0, n, :, cols[0]] = jnp.broadcast_to(total, (8, LANES))
 
 
-def attend_back(qkv, probs, upstream):
+def attend_back(qkv, probs, upstream, after):
     rows, cols = qkv.shape
     half = cols // 2
     quarter = half // 3
@@ -199,36 +205,158 @@
             pl.BlockSpec((rows, half), lambda i: (0, i)),
             pl.BlockSpec((heads, rows, rows), lambda i: (i, 0, 0)),
             pl.BlockSpec((rows, quarter), lambda i: (0, i)),
-        ],
+        ]
+        + [pl.BlockSpec(memory_space=pl.ANY)] * len(after),
         out_specs=[pl.BlockSpec((rows, half), lambda i: (0, i)), pl.BlockSpec((1, 2, 8, quarter), lambda i: (i, 0, 0, 0))],
         compiler_params=pltpu.CompilerParams(vmem_limit_bytes=48 << 20),
         cost_estimate=pl.CostEstimate(flops=20_000_000_000, bytes_accessed=8 << 20, transcendentals=0),
         name="attend_back",
-    )(qkv, probs, upstream)
-
-
-def scatter_sum(grad, dp_count):
-    rows, _, cols = grad.shape
+    )(qkv, probs, upstream, *after)
+
+
+def grad_kernel(lefts, place, *refs):
+    sources = refs[: 2 * lefts]
+    rights = refs[2 * lefts : 4 * lefts]
+    outs = refs[-4 - lefts : -lefts]
+    turned = refs[-lefts:]
+    i = pl.program_id(0)
+    x = place[1]
+    rows, width = sources[0].shape
+    piece = width // 8
+
+    @pl.when(i == 0)
+    def _():
+        for n in range(lefts):
+            for at in range(8):
+                high, far_x, low = at // 4, (at // 2) % 2, at % 2
+                block = (2 * high + low) * 2 + lax.rem(x + far_x, 2)
+                cols = pl.ds(pl.multiple_of(block * piece, piece), piece)
+                for far in range(2):
+                    turned[n][at * piece : (at + 1) * piece, far * rows : (far + 1) * rows] = sources[2 * n + far][:, cols].T
+
+    def work(n):
+        right = jnp.concatenate([rights[2 * n][...], rights[2 * n + 1][...]], 0)
+        out = dot(turned[n][...], right, 1, 0).astype(bf16)
+        out = out.reshape(8, piece, out.shape[1])
+
+        @pl.when(i < 4)
+        def _():
+            outs[0][...] = out[:4]
+
+        @pl.when(i >= 4)
+        def _():
+            outs[1][...] = out[:4]
+
+        outs[2][0] = out[4:6]
+        outs[3][0] = out[6:]
+
+    if lefts == 1:
+        work(0)
+    else:
+        last = lax.rem(i, 4) == 3
+        pl.when(jnp.logical_not(last))(lambda: work(0))
+        pl.when(last)(lambda: work(1))
+
+
+def weight_grad(place, pairs):
+    rows, width = pairs[0][0].shape
+    piece = width // 8
+    whole = pl.BlockSpec((rows, width), lambda i: (0, 0))
+    if len(pairs) == 1:
+        maps = [lambda i: (0, i)]
+    else:
+        maps = [lambda i: (0, (i // 4) * 3 + jnp.minimum(i % 4, 2)), lambda i: (0, i // 4)]
+    right_specs = [pl.BlockSpec((rows, 256), m) for m in maps for _ in range(2)]
+    lefts = [v for p in pairs for v in p[:2]]
+    rights = [v for p in pairs for v in p[2:]]
+    out_specs = [
+        pl.BlockSpec((4, piece, 256), lambda i: (0, 0, jnp.minimum(i, 3))),
+        pl.BlockSpec((4, piece, 256), lambda i: (0, 0, jnp.maximum(i, 4) - 4)),
+        pl.BlockSpec((1, 2, piece, 256), lambda i: (i // 4, 0, 0, i % 4)),
+        pl.BlockSpec((1, 2, piece, 256), lambda i: (i // 4, 0, 0, i % 4)),
+    ]
+    return pl.pallas_call(
+        functools.partial(grad_kernel, len(pairs)),
+        grid=(8,),
+        out_shape=[jax.ShapeDtypeStruct((4, piece, 1024), bf16)] * 2 + [jax.ShapeDtypeStruct((2, 2, piece, 1024), bf16)] * 2,
+        in_specs=[pl.BlockSpec(memory_space=pltpu.SMEM)] + [whole] * len(lefts) + right_specs,
+        out_specs=out_specs,
+        scratch_shapes=[pltpu.VMEM((width, 2 * rows), bf16)] * len(pairs),
+        compiler_params=pltpu.CompilerParams(vmem_limit_bytes=40 << 20),
+        cost_estimate=pl.CostEstimate(flops=4 << 30, bytes_accessed=12 << 20, transcendentals=0),
+        name="weight_grad",
+    )(place, *lefts, *rights)
+
+
+def sum_one_kernel(one, got_one, two, got_two, keep_one, send_one, keep_two, send_two):
+    for mine, got, keep, send in ((one, got_one, keep_one, send_one), (two, got_two, keep_two, send_two)):
+        keep[...] = add(mine[0], got[0])
+        send[...] = add(mine[1], got[1])
+
+
+def sum_one(one, got_one, two, got_two):
+    _, piece, cols = one.shape
+    four = (2, 2, piece, cols)
+    block = pl.BlockSpec((2, 2, piece, 256), lambda i: (0, 0, 0, i))
+    return pl.pallas_call(
+        sum_one_kernel,
+        grid=(cols // 256,),
+        out_shape=[jax.ShapeDtypeStruct(four[1:], bf16)] * 4,
+        in_specs=[block] * 4,
+        out_specs=[pl.BlockSpec((2, piece, 256), lambda i: (0, 0, i))] * 4,
+        compiler_params=pltpu.CompilerParams(vmem_limit_bytes=24 << 20),
+        cost_estimate=pl.CostEstimate(flops=1 << 20, bytes_accessed=6 << 20, transcendentals=0),
+        name="sum_one",
+    )(one.reshape(four), got_one.reshape(four), two, got_two)
+
+
+def sum_two_kernel(place, one, got_one, two, got_two, own, *rest):
+    sends, line = rest[:3], rest[3]
+    line[:2] = add(one[...], got_one[...])
+    line[2:] = add(two[...], got_two[...])
+    own[...] = line[place[0]]
+    for k in range(1, 4):
+        sends[k - 1][...] = line[lax.rem(place[0] + k, 4)]
+
+
+def sum_two(place, one, got_one, two, got_two):
+    _, piece, cols = one.shape
+    block = pl.BlockSpec((2, piece, 256), lambda i: (0, 0, i))
+    return pl.pallas_call(
+        sum_two_kernel,
+        grid=(cols // 256,),
+        out_shape=[jax.ShapeDtypeStruct((piece, cols), bf16)] * 4,
+        in_specs=[pl.BlockSpec(memory_space=pltpu.SMEM)] + [block] * 4,
+        out_specs=[pl.BlockSpec((piece, 256), lambda i: (0, i))] * 4,
+        scratch_shapes=[pltpu.VMEM((4, piece, 256), bf16)],
+        compiler_params=pltpu.CompilerParams(vmem_limit_bytes=24 << 20),
+        cost_estimate=pl.CostEstimate(flops=1 << 20, bytes_accessed=3 << 20, transcendentals=0),
+        name="sum_two",
+    )(place, one, got_one, two, got_two)
+
+
+def first_sends(place, pairs, dp_count):
     if dp_count != 8:
-        t = lax.axis_index("tp")
+        grads = []
+        for left, left_far, right, right_far in pairs:
+            both = dot(jnp.concatenate([left, left_far], 0), jnp.concatenate([right, right_far], 0), 0, 0)
+            grads.append(both.astype(bf16).reshape(both.shape[0], 2, -1))
+        return (jnp.concatenate(grads, 2),)
+    keep_one, send_one, keep_two, send_two = weight_grad(place, pairs)
+    return (keep_one, send_one, keep_two, send_two)
+
+
+def scatter_sum(place, parts, dp_count):
+    if dp_count != 8:
+        (grad,) = parts
         mine = add(grad[:, 0], swap(grad[:, 1], "tp"))
         return lax.psum_scatter(mine, "dp", scatter_dimension=0, tiled=True).astype(f32)
-    d = lax.axis_index("dp")
-    x, z = d % 2, d // 2
-    blocks = grad.reshape(2, 2, 2, rows // 8, 2, cols)
-    first, second = blocks[0], blocks[1]
-    got = swap(first[:, :, :, 1], "tp")
-    got_b = swap_x(take(second, 1 - x, 1))
-    first = add(first[:, :, :, 0], got)
-    second = add(take(second, x, 1), got_b)
-    got = swap_x(take(first, 1 - x, 1))
-    got_b = swap(second[:, :, 1], "tp")
-    first = add(take(first, x, 1), got)
-    second = add(second[:, :, 0], got_b)
-    line = jnp.concatenate([first, second], axis=0)
-    total = take(line, z).astype(f32)
-    for step in range(1, 4):
-        total = total + shift_z(take(line, (z + step) % 4), step).astype(f32)
+    keep_one, send_one, keep_two, send_two = parts
+    keep_one, send_one, keep_two, send_two = sum_one(keep_one, swap(send_one, "tp"), keep_two, swap_x(send_two))
+    own, *sends = sum_two(place, keep_one, swap_x(send_one), keep_two, swap(send_two, "tp"))
+    total = own.astype(f32)
+    for k in range(1, 4):
+        total = total + shift_z(sends[k - 1], k).astype(f32)
     return total
 
 
@@ -245,20 +373,22 @@
 
     one = jnp.stack([query_weight, key_weight, value_weight, out_weight.T], 1)
     one = one.reshape(piece_rows, 4, 2, -1).transpose(2, 0, 1, 3).reshape(2, piece_rows, -1)
-    up = up_weight.reshape(piece_rows, 2, -1).transpose(1, 0, 2)
-    down = down_weight.T.reshape(piece_rows, 2, -1).transpose(1, 0, 2)
-    packed = jnp.stack([one, up, down], 1).astype(bf16)
-    pieces = order(c, take(packed, c), swap(take(packed, 1 - c), "ctx"), 1)
-    unit = pieces.shape[2]
+    one = one.astype(bf16)
+    piece = order(c, take(one, c), swap(take(one, 1 - c), "ctx"), 0)
+    unit = piece.shape[1]
     quarter = unit // 4
-    whole = ((0, unit),)
-    qkv_mine, out_mine = gather_weights(pieces[0], ((0, 3 * quarter), (3 * quarter, quarter)), place, dp_count)
+    qkv_mine, out_mine = gather_weights(piece, ((0, 3 * quarter), (3 * quarter, quarter)), place, dp_count)
     w_qkv = (qkv_mine, swap(qkv_mine, "ctx"))
     w_out = (out_mine, swap(out_mine, "ctx"))
-    (up_mine,) = gather_weights(pieces[1], whole, place, dp_count)
-    w_up = (up_mine, swap(up_mine, "ctx"))
-    (down_mine,) = gather_weights(pieces[2], whole, place, dp_count)
-    w_down = (down_mine, swap(down_mine, "ctx"))
+    rest = jnp.concatenate([up_weight.astype(bf16), down_weight.T.astype(bf16)], 1)
+    rest = lax.all_gather(rest, ("tp", "dp", "ctx"), axis=0, tiled=True).reshape(2, width, 2, 2, unit)
+
+    def columns(group, core):
+        parts = [lax.dynamic_slice(rest, (tp, 0, group, core, 0), (1, width, 1, 1, unit)).reshape(width, unit) for tp in (t, 1 - t)]
+        return jnp.concatenate(parts, 1)
+
+    w_up = (columns(0, c), columns(0, 1 - c))
+    w_down = (columns(1, c), columns(1, 1 - c))
 
     biases = jnp.concatenate([query_bias, value_bias, up_bias])
     biases = jnp.stack([biases, swap(biases, "tp")])
@@ -306,34 +436,30 @@
     up_bias_term = jnp.stack([jnp.sum(g.astype(f32), axis=0) for g in grad_pre])
 
     def far(values):
-        return jnp.concatenate([values, swap(values, "ctx")], 0)
-
-    def mine_and_far(pair):
-        return jnp.concatenate([pair[0], swap(pair[1], "ctx")], 0)
-
-    def grads(left, right):
-        return dot(left, right, 0, 0).astype(bf16)
-
-    down_grad = grads(far(grad_mixed), mine_and_far(hidden)).reshape(width, 2, -1)
-    up_grad = grads(far(normed_low), mine_and_far(grad_pre)).reshape(width, 2, -1)
-    down_total = scatter_sum(down_grad, dp_count)
-    up_total = scatter_sum(up_grad, dp_count)
+        return swap(values, "ctx")
+
+    down_parts = first_sends(place, [(grad_mixed, far(grad_mixed), hidden[0], far(hidden[1]))], dp_count)
+    up_parts = first_sends(place, [(normed_low, far(normed_low), grad_pre[0], far(grad_pre[1]))], dp_count)
+    down_total = scatter_sum(place, down_parts, dp_count)
+    up_total = scatter_sum(place, up_parts, dp_count)
 
     grad_normed = grad_two + dot(grad_pre[0], w_up[0], 1, 1) + dot(grad_pre[1], w_up[1], 1, 1)
     grad_one, attn_gain_term, attn_shift_term = norm_backward(grad_normed, unit_one, inverse_one, attn_gain)
     grad_attended = grad_one.astype(bf16)
     out_bias_term = jnp.sum(grad_one, axis=0)
-    grad_attended, down_grad, up_grad = lax.optimization_barrier((grad_attended, down_grad, up_grad))
     grad_context = [dot(grad_attended, w_out[r], 1, 0).astype(bf16) for r in range(2)]
-    back = [attend_back(qkv[r], probs[r], grad_context[r]) for r in range(2)]
+    back = [attend_back(qkv[r], probs[r], grad_context[r], (down_parts[-1], up_parts[-1])) for r in range(2)]
     grad_qkv = [b[0] for b in back]
     sums = jnp.stack([b[1] for b in back])[:, :, :, 0]
     sent_back = dot(grad_qkv[0], w_qkv[0], 1, 1) + dot(grad_qkv[1], w_qkv[1], 1, 1)
     input_grad = (grad_one + sent_back).astype(bf16)
 
-    qkv_grad = grads(jnp.concatenate([flat, flat_far], 0), mine_and_far(grad_qkv)).reshape(width, 2, -1)
-    out_grad = grads(far(grad_attended), mine_and_far(context)).reshape(width, 2, -1)
-    one_total = scatter_sum(jnp.concatenate([qkv_grad, out_grad], 2), dp_count)
+    one_parts = first_sends(
+        place,
+        [(flat, flat_far, grad_qkv[0], far(grad_qkv[1])), (grad_attended, far(grad_attended), context[0], far(context[1]))],
+        dp_count,
+    )
+    one_total = scatter_sum(place, one_parts, dp_count)
 
     def settle(values):
         values = jnp.where(c == 0, values, values[::-1])

time: 909 us -> 498 us (0.55)
  Pallas kernels: 415 us -> 74.6 us
  starting transfers between devices: 101 us -> 42.3 us
  local copies, waits for them, and re-layouts: 67.9 us -> 109 us
  matrix products: 85.9 us -> 57 us
  other arithmetic: 50.6 us -> 28.4 us
    pallas_call x3 -> x1, Pallas kernels: 387 us -> 4.51 us  [gather_weights(): pl.pallas_call(functools.partial(assemble_kernel, cuts), out_shape=[jax.S...]
    ppermute x18 -> x12, starting transfers between devices: 69.3 us -> 17.2 us  [shift_z(): lax.ppermute(values, 'dp', [(i, (i + 2 * step) % 8) for i in range(8)])]
    pallas_call x0 -> x9, Pallas kernels: none -> 39.8 us  [the longest x3 30 us: weight_grad(): pl.pallas_call(functools.partial(grad_kernel, len(pairs)), grid=(8,), out...]
    dynamic_slice x0 -> x1, local copies, waits for them, and re-layouts: none -> 38.3 us  [columns(): lax.dynamic_slice(rest, (tp, 0, group, core, 0), (1, width, 1, 1, unit))]
    ppermute x18 -> x12, waiting for transfers between devices: 45.6 us -> 82.3 us  [shift_z(): lax.ppermute(values, 'dp', [(i, (i + 2 * step) % 8) for i in range(8)])]
    dot_general x20 -> x16, matrix products: 85.9 us -> 57 us  [dot(): lax.dot_general(left, right, (((left_dim,), (right_dim,)), ((), ())), pre...]
    ppermute x31 -> x25, waiting for transfers between devices: 86.2 us -> 61 us  [swap(): return lax.ppermute(values, axis, [(0, 1), (1, 0)])]
    reshape x4 -> x1, local copies, waits for them, and re-layouts: 2.62 us -> 27.7 us  [body(): lax.all_gather(rest, ('tp', 'dp', 'ctx'), axis=0, tiled=True)]
  transfers between devices with their start and end apart: 62 -> 47, of which waited for: 17 -> 15; matrix products, arithmetic and copies ran while one was open for 16% -> 34% of each run, Pallas kernels for 46% -> 15%
where the time goes in v3:
time: 498 us; the launch traced here: 493 us
  waiting for transfers between devices  166 us (33%)
  local copies, waits for them, and re-layouts  109 us (22%)
  Pallas kernels  74.6 us (15%)
  matrix products  57 us (11%)
  starting transfers between devices  42.3 us (8%)
  other arithmetic  28.4 us (6%)
  between operations  15.7 us (3%)
    ppermute x12, waiting for transfers between devices, shift_z(): lax.ppermute(values, 'dp', [(i, (i + 2 * step) % 8) for i in range(8)])  82.3 us
    ppermute x25, waiting for transfers between devices, swap(): return lax.ppermute(values, axis, [(0, 1), (1, 0)])  61 us
    dot_general x16, matrix products, dot(): lax.dot_general(left, right, (((left_dim,), (right_dim,)), ((), ())), pre...  57 us
    dynamic_slice x1, local copies, waits for them, and re-layouts, columns(): lax.dynamic_slice(rest, (tp, 0, group, core, 0), (1, width, 1, 1, unit))  38.3 us
    pallas_call x3, Pallas kernels, weight_grad(): pl.pallas_call(functools.partial(grad_kernel, len(pairs)), grid=(8,), out...  30 us
    unnamed x158, local copies, waits for them, and re-layouts  28.6 us
    reshape x1, local copies, waits for them, and re-layouts, body(): lax.all_gather(rest, ('tp', 'dp', 'ctx'), axis=0, tiled=True)  27.7 us
    ppermute x8, waiting for transfers between devices, swap_x(): return lax.ppermute(values, 'dp', [(i, i ^ 1) for i in range(8)])  21.7 us
  transfers between devices with their start and end apart: 47, of which 15 were waited for; matrix products, arithmetic and copies ran while one was open for 34% of the time, Pallas kernels for 15%

profile of v3, /device:TPU:0, one launch (start us, length us, event | category | flops | bytes accessed | tf_op | source)
XLA Modules:
  0.0 492.8 jit_solution(15026585793573606238)
XLA Ops:
  21.0 5.3 %collective-permute-done.2 = bf16[128,1024]{1,0:T(8,128)(2,1)S(1)} collective-permute-done((bf16[128,1024]{1,0:T(8,128)(2,1)S(1)}, bf16[128,1024]{1,0:T(8,128)(2,1)S(1)}, u32[]{:S(2)}, u32[]{:S(2)}) %collective-permute-start.2) | collective-permute-done | bytes 262176 | tf_op jit(solution)/shard_map/ppermute | solution.py:47
  27.9 10.0 %collective-permute-done.6 = bf16[128,1024]{1,0:T(8,128)(2,1)S(1)} collective-permute-done((bf16[128,1024]{1,0:T(8,128)(2,1)S(1)}, bf16[128,1024]{1,0:T(8,128)(2,1)S(1)}, u32[]{:S(2)}, u32[]{:S(2)}) %collective-permute-start.6) | collective-permute-done | bytes 262176 | tf_op jit(solution)/shard_map/ppermute | solution.py:47
  37.9 15.7 %collective-permute-done.5 = bf16[128,1024]{1,0:T(8,128)(2,1)S(1)} collective-permute-done((bf16[128,1024]{1,0:T(8,128)(2,1)S(1)}, bf16[128,1024]{1,0:T(8,128)(2,1)S(1)}, u32[]{:S(2)}, u32[]{:S(2)}) %collective-permute-start.5) | collective-permute-done | bytes 262176 | tf_op jit(solution)/shard_map/ppermute | solution.py:47
  59.8 17.1 %collective-permute-done.7 = bf16[2,128,1024]{2,1,0:T(8,128)(2,1)} collective-permute-done((bf16[2,128,1024]{2,1,0:T(8,128)(2,1)S(1)}, bf16[2,128,1024]{2,1,0:T(8,128)(2,1)}, u32[]{:S(2)}, u32[]{:S(2)}) %collective-permute-start.7) | collective-permute-done | bytes 524320 | tf_op jit(solution)/shard_map/ppermute | solution.py:39
  80.0 22.3 %collective-permute-done.4.one_y = bf16[2,2,128,1024]{3,2,1,0:T(8,128)(2,1)S(1)} collective-permute-done((bf16[2,2,128,1024]{3,2,1,0:T(8,128)(2,1)S(1)}, bf16[2,2,128,1024]{3,2,1,0:T(8,128)(2,1)S(1)}, u32[]{:S(2)}, u32[]{:S(2)}) %collective-permute-start.4) | collective-permute-done | bytes 1048608 | tf_op jit(solution)/shard_map/ppermute | solution.py:39
  103.3 7.2 %collective-permute-done.8.two_x = bf16[2,2,128,1024]{3,2,1,0:T(8,128)(2,1)} collective-permute-done((bf16[2,2,128,1024]{3,2,1,0:T(8,128)(2,1)S(1)}, bf16[2,2,128,1024]{3,2,1,0:T(8,128)(2,1)}, u32[]{:S(2)}, u32[]{:S(2)}) %collective-permute-start.8) | collective-permute-done | bytes 1048608 | tf_op jit(solution)/shard_map/ppermute | solution.py:43
  111.8 4.5 assemble.1
  124.9 6.7 %attend.2 = (bf16[512,512]{1,0:T(8,128)(2,1)S(1)}, bf16[8,512,512]{2,1,0:T(8,128)(2,1)}) custom-call(bf16[512,1536]{1,0:T(8,128)(2,1)S(1)} %fusion.10.qkv, s32[512,1]{1,0:T(8,128)S(1)} %broadcast_select_fusion.seg_keys, s32[1,512]{1,0:T(1,128)S(1)} %get-tuple-element.174.seg_queries), custom_call_target="tpu_custom_call" | custom-call | flops 12000000000 | bytes 8388608 | tf_op jit(solution)/shard_map/attend/pallas_call | solution.py:147
  136.9 6.6 %attend.3 = (bf16[512,512]{1,0:T(8,128)(2,1)}, bf16[8,512,512]{2,1,0:T(8,128)(2,1)}) custom-call(bf16[512,1536]{1,0:T(8,128)(2,1)S(1)} %fusion.11.qkv, s32[512,1]{1,0:T(8,128)S(1)} %broadcast_select_fusion.seg_keys, s32[1,512]{1,0:T(1,128)S(1)} %get-tuple-element.174.seg_queries), custom_call_target="tpu_custom_call" | custom-call | flops 12000000000 | bytes 8388608 | tf_op jit(solution)/shard_map/attend/pallas_call | solution.py:147
  149.3 27.7 %reshape.306 = bf16[2,1024,2,2,1024]{4,3,2,1,0:T(2,128)(2,1)} reshape(bf16[2048,4096]{1,0:T(8,128)(2,1)} %all-gather.3.cloned.1.call-done) | data formatting | bytes 33554432 | tf_op jit(solution)/shard_map/reshape | solution.py:384
  177.0 38.3 %constant_dynamic-slice_fusion.7 = (bf16[1,1024,1,1,1024]{4,3,2,1,0:T(2,128)(2,1)S(1)}, bf16[1,1024,1,1,1024]{4,3,2,1,0:T(2,128)(2,1)S(1)}, bf16[1,1024,1,1,1024...) fusion(bf16[2,1024,2,2,1024]{4,3,2,1,0:T(2,128)(2,1)} %reshape., ...), kind=kLoop, calls=%fused_computation.126 | loop fusion | bytes 33554448 | tf_op jit(solution)/shard_map/dynamic_slice | solution.py:387
  224.1 6.2 %multiply_convert_fusion.2 = (bf16[512,2048]{1,0:T(8,128)(2,1)}, f32[512,2048]{1,0:T(8,128)}) fusion(f32[2048]{0:T(1024)S(1)} %bitcast.270, bf16[512,1024]{1,0:T(8,128)(2,1)} %fusion.25.refs_0_, bf16[1024,1024]{1,0:T(8,128)(2,1)S(1)} %bitcast.208, bf16[1024,1024]{1,0:T(8,128)(2,1)S(1)} %bitcast.210), kind=kOutput, calls=%fused_computation.20 | convolution fusion | flops 2162163712 | bytes 11542528 | tf_op jit(solution)/shard_map/dot_general | solution.py:21
  230.6 3.9 fusion.15
  234.5 5.8 %multiply_convert_fusion.3 = (bf16[512,2048]{1,0:T(8,128)(2,1)S(1)}, f32[512,2048]{1,0:T(8,128)}) fusion(f32[2048]{0:T(1024)S(1)} %bitcast.268, bf16[512,1024]{1,0:T(8,128)(2,1)} %fusion.25.refs_0_, bf16[1024,1024]{1,0:T(8,128)(2,1)S(1)} %bitcast.204, bf16[1024,1024]{1,0:T(8,128)(2,1)S(1)} %bitcast.206), kind=kOutput, calls=%fused_computation.22 | convolution fusion | flops 2162163712 | bytes 11542528 | tf_op jit(solution)/shard_map/dot_general | solution.py:21
  247.5 5.2 %convert_reduce_fusion = (f32[2048]{0:T(1024)S(1)}, bf16[512,2048]{1,0:T(8,128)(2,1)}) fusion(f32[512,2048]{1,0:T(8,128)S(1)} %copy-done.63, f32[2048]{0:T(1024)S(1)} %bitcast.271, bf16[512,1024]{1,0:T(8,128)(2,1)S(1)} %convert_element_type.128.refs_0_, bf16[1024,1024]{1,0:T(8,128)(2,1)S(1)} %bitcast.217, bf16[1024,1024]{1,0:T(8,128)(2,1)S(1)} %bitcast.219), kind=kOutput, calls=%fused_computation.16 | convolution fusion | flops 2171598848 | bytes 11550720 | tf_op jit(solution)/shard_map/dot_general | solution.py:21
  252.7 4.1 fusion.16
  257.2 4.7 convert_reduce_fusion.1
  261.9 4.4 multiply_reduce_fusion
  273.9 10.1 %weight_grad.3 = (bf16[4,128,1024]{2,1,0:T(8,128)(2,1)S(1)}, bf16[4,128,1024]{2,1,0:T(8,128)(2,1)}, bf16[2,2,128,1024]{3,2,1,0:T(8,128)(2,1)S(1)}, bf16[2,2,128,1024]{3,2,1,0:T(8,128)(2,1)}) custom-call(s32[2]{0:T(128)S(1)} %pad_add_fusion.1.place, bf16[512,1024]{1,0:T(8,128)(2,1)S(1)} %convert_element_type.128.refs_0_, ...), custom_call_target="tpu_custom_call" | custom-call | flops 4294967296 | bytes 12582912 | tf_op jit(solution)/shard_map/weight_grad/pallas_call | solution.py:278
  288.8 9.8 %weight_grad.4 = (bf16[4,128,1024]{2,1,0:T(8,128)(2,1)S(1)}, bf16[4,128,1024]{2,1,0:T(8,128)(2,1)S(1)}, bf16[2,2,128,1024]{3,2,1,0:T(8,128)(2,1)S(1)}, bf16[2,2,128,1024]{3,2,1,0:T(8,128)(2,1)S(1)}) custom-call(s32[2]{0:T(128)S(1)} %pad_add_fusion.1.place, bf16[512,1024]{1,0:T(8,128)(2,1)} %fusion.25.refs_0_, ...), custom_call_target="tpu_custom_call" | custom-call | flops 4294967296 | bytes 12582912 | tf_op jit(solution)/shard_map/weight_grad/pallas_call | solution.py:278
  301.6 8.8 %attend_back.3 = (bf16[512,1536]{1,0:T(8,128)(2,1)}, f32[2,2,8,256]{3,2,1,0:T(8,128)S(1)}) custom-call(bf16[512,1536]{1,0:T(8,128)(2,1)S(1)} %copy-done.23, bf16[8,512,512]{2,1,0:T(8,128)(2,1)} %get-tuple-element.71.probs, bf16[512,512]{1,0:T(8,128)(2,1)S(1)} %convolution_convert_fusion.upstream, bf16[2,2,128,1024]{3,2,1,0:T(8,128)(2,1)} %get-tuple-element.68.rest_0_, ...), custom_call_target="tpu_custom_call" | custom-call | flops 20000000000 | bytes 8388608 | tf_op jit(solution)/shard_map/attend_back/pallas_call | solution.py:200
  310.5 8.2 %attend_back.2 = (bf16[512,1536]{1,0:T(8,128)(2,1)S(1)}, f32[2,2,8,256]{3,2,1,0:T(8,128)S(1)}) custom-call(bf16[512,1536]{1,0:T(8,128)(2,1)S(1)} %copy-done.21, bf16[8,512,512]{2,1,0:T(8,128)(2,1)} %get-tuple-element.67.probs, bf16[512,512]{1,0:T(8,128)(2,1)S(1)} %convolution_convert_fusion.1.upstream, bf16[2,2,128,1024]{3,2,1,0:T(8,128)(2,1)} %get-tuple-element.68.rest_0_, ...), custom_call_target="tpu_custom_call" | custom-call | flops 20000000000 | bytes 8388608 | tf_op jit(solution)/shard_map/attend_back/pallas_call | solution.py:200
  324.9 10.1 %weight_grad.5 = (bf16[4,128,1024]{2,1,0:T(8,128)(2,1)S(1)}, bf16[4,128,1024]{2,1,0:T(8,128)(2,1)S(1)}, bf16[2,2,128,1024]{3,2,1,0:T(8,128)(2,1)S(1)}, bf16[2,2,128,1024]{3,2,1,0:T(8,128)(2,1)S(1)}) custom-call(s32[2]{0:T(128)S(1)} %pad_add_fusion.1.place, bf16[512,1024]{1,0:T(8,128)(2,1)S(1)} %copy-done.2, bf16[512,1024]{1,0:T(8,128)(2,1)S(1)} %copy-done.3, ...), custom_call_target="tpu_custom_call" | custom-call | flops 4294967296 | bytes 12582912 | tf_op jit(solution)/shard_map/weight_grad/pallas_call | solution.py:278
  337.7 4.2 fusion.53
  342.1 3.9 add_convert_fusion
  352.9 21.4 %collective-permute-done.23 = bf16[4,128,1024]{2,1,0:T(8,128)(2,1)S(1)} collective-permute-done((bf16[4,128,1024]{2,1,0:T(8,128)(2,1)S(1)}, bf16[4,128,1024]{2,1,0:T(8,128)(2,1)S(1)}, u32[]{:S(2)}, u32[]{:S(2)}) %collective-permute-start.23) | collective-permute-done | bytes 1048608 | tf_op jit(solution)/shard_map/ppermute | solution.py:39
  378.0 7.4 %collective-permute-done.39.got_one = bf16[2,128,1024]{2,1,0:T(8,128)(2,1)S(1)} collective-permute-done((bf16[2,128,1024]{2,1,0:T(8,128)(2,1)S(1)}, bf16[2,128,1024]{2,1,0:T(8,128)(2,1)S(1)}, u32[]{:S(2)}, u32[]{:S(2)}) %collective-permute-start.39) | collective-permute-done | bytes 524320 | tf_op jit(solution)/shard_map/ppermute | solution.py:43
  389.6 7.1 %collective-permute-done.32.got_one = bf16[2,128,1024]{2,1,0:T(8,128)(2,1)S(1)} collective-permute-done((bf16[2,128,1024]{2,1,0:T(8,128)(2,1)S(1)}, bf16[2,128,1024]{2,1,0:T(8,128)(2,1)S(1)}, u32[]{:S(2)}, u32[]{:S(2)}) %collective-permute-start.32) | collective-permute-done | bytes 524320 | tf_op jit(solution)/shard_map/ppermute | solution.py:43
  402.4 14.3 %collective-permute-done.42 = bf16[128,1024]{1,0:T(8,128)(2,1)S(1)} collective-permute-done((bf16[128,1024]{1,0:T(8,128)(2,1)S(1)}, bf16[128,1024]{1,0:T(8,128)(2,1)S(1)}, u32[]{:S(2)}, u32[]{:S(2)}) %collective-permute-start.42) | collective-permute-done | bytes 262176 | tf_op jit(solution)/shard_map/ppermute | solution.py:47
  424.3 4.3 collective-permute-start.29
  428.6 22.7 %collective-permute-done.35 = bf16[128,1024]{1,0:T(8,128)(2,1)S(1)} collective-permute-done((bf16[128,1024]{1,0:T(8,128)(2,1)S(1)}, bf16[128,1024]{1,0:T(8,128)(2,1)S(1)}, u32[]{:S(2)}, u32[]{:S(2)}) %collective-permute-start.35) | collective-permute-done | bytes 262176 | tf_op jit(solution)/shard_map/ppermute | solution.py:47
  451.6 12.3 %collective-permute-done.28 = bf16[128,1024]{1,0:T(8,128)(2,1)S(1)} collective-permute-done((bf16[128,1024]{1,0:T(8,128)(2,1)S(1)}, bf16[128,1024]{1,0:T(8,128)(2,1)S(1)}, u32[]{:S(2)}, u32[]{:S(2)}) %collective-permute-start.28) | collective-permute-done | bytes 262176 | tf_op jit(solution)/shard_map/ppermute | solution.py:47
  (359 shorter events, 136.9 us)
Async XLA Ops:
  7.2 142.1 %all-gather.3.cloned.1.call-start = ((), (), s32[]{:S(2)}) async-start(), calls=%async_computation | async-start | bytes 17301504 | tf_op jit(solution)/shard_map/all_gather | solution.py:384
  10.5 461.3 %all-gather.5.cloned.1.call-start = ((), (), s32[]{:S(2)}) async-start(), calls=%async_computation.1 | async-start | bytes 1622016 | tf_op jit(solution)/shard_map/all_gather | solution.py:472
  12.6 67.4 %collective-permute-start.9 = (f32[3072]{0:T(1024)S(1)}, f32[3072]{0:T(1024)S(1)}, u32[]{:S(2)}, u32[]{:S(2)}) collective-permute-start(f32[3072]{0:T(1024)S(1)} %constant_dynamic-update-slice_fusion), channel_id=1, source_target_pairs={{0,1},{1,0},{2,3},{3,2},{4,5},{5,4},{6,7},{7,6},{8,9},{9,8},{10,11... | collective-permute-start | bytes 36872 | tf_op jit(solution)/shard_map/ppermute | solution.py:39
  19.3 34.3 %collective-permute-start.5 = (bf16[128,1024]{1,0:T(8,128)(2,1)S(1)}, bf16[128,1024]{1,0:T(8,128)(2,1)S(1)}, u32[]{:S(2)}, u32[]{:S(2)}) collective-permute-start(bf16[128,1024]{1,0:T(8,128)(2,1)S(1)} %maximum_select_fusion.6), channel_id=1, source_target_pairs={{0,16},{4,20},{8,24},{12,28},{16,0},{20,4},{24,8},{28,12},{1,17},{... | collective-permute-start | bytes 786440 | tf_op jit(solution)/shard_map/ppermute | solution.py:47
  26.4 32.4 %collective-permute-start.3 = (bf16[2,128,1024]{2,1,0:T(8,128)(2,1)S(1)}, bf16[2,128,1024]{2,1,0:T(8,128)(2,1)S(1)}, u32[]{:S(2)}, u32[]{:S(2)}) collective-permute-start(bf16[2,128,1024]{2,1,0:T(8,128)(2,1)S(1)} %get-tuple-element.155), channel_id=1, source_target_pairs={{0,4},{4,0},{8,12},{12,8},{16,20},{20,16},{24,28},{28,24},{1,5},{5... | collective-permute-start | bytes 1572872 | tf_op jit(solution)/shard_map/ppermute | solution.py:43
  57.0 59.9 %collective-permute-start = (bf16[3,256,1024]{2,1,0:T(8,128)(2,1)}, bf16[3,256,1024]{2,1,0:T(8,128)(2,1)}, u32[]{:S(2)}, u32[]{:S(2)}) collective-permute-start(bf16[3,256,1024]{2,1,0:T(8,128)(2,1)} %pad_maximum_fusion.12), channel_id=1, source_target_pairs={{0,2},{2,0},{1,3},{3,1},{4,6},{6,4},{5,7},{7,5},{8,10},{10,8},{9,1... | collective-permute-start | bytes 4718600 | tf_op jit(solution)/shard_map/ppermute | solution.py:39
  58.9 43.5 %collective-permute-start.4 = (bf16[2,2,128,1024]{3,2,1,0:T(8,128)(2,1)S(1)}, bf16[2,2,128,1024]{3,2,1,0:T(8,128)(2,1)S(1)}, u32[]{:S(2)}, u32[]{:S(2)}) collective-permute-start(bf16[2,2,128,1024]{3,2,1,0:T(8,128)(2,1)S(1)} %pad_maximum_fusion.19.one), channel_id=1, source_target_pairs={{0,1},{1,0},{2,3},{3,2},{4,5},{5,4},{6,7},{7,6},{8,9},{9,8},{10,11... | collective-permute-start | bytes 3145736 | tf_op jit(solution)/shard_map/ppermute | solution.py:39
  78.2 32.3 %collective-permute-start.8 = (bf16[2,2,128,1024]{3,2,1,0:T(8,128)(2,1)S(1)}, bf16[2,2,128,1024]{3,2,1,0:T(8,128)(2,1)}, u32[]{:S(2)}, u32[]{:S(2)}) collective-permute-start(bf16[2,2,128,1024]{3,2,1,0:T(8,128)(2,1)S(1)} %pad_maximum_fusion.20.two), channel_id=1, source_target_pairs={{0,4},{4,0},{8,12},{12,8},{16,20},{20,16},{24,28},{28,24},{1,5},{5... | collective-permute-start | bytes 3145736 | tf_op jit(solution)/shard_map/ppermute | solution.py:43
  120.7 22.8 %collective-permute-start.11 = (bf16[1024,512]{1,0:T(8,128)(2,1)S(1)}, bf16[1024,512]{1,0:T(8,128)(2,1)S(1)}, u32[]{:S(2)}, u32[]{:S(2)}) collective-permute-start(bf16[1024,512]{1,0:T(8,128)(2,1)S(1)} %get-tuple-element.65), channel_id=1, source_target_pairs={{0,2},{2,0},{1,3},{3,1},{4,6},{6,4},{5,7},{7,5},{8,10},{10,8},{9,1... | collective-permute-start | bytes 3145736 | tf_op jit(solution)/shard_map/ppermute | solution.py:39
  143.4 177.5 %collective-permute-start.22 = (bf16[512,512]{1,0:T(8,128)(2,1)}, bf16[512,512]{1,0:T(8,128)(2,1)}, u32[]{:S(2)}, u32[]{:S(2)}) collective-permute-start(bf16[512,512]{1,0:T(8,128)(2,1)} %get-tuple-element.66), channel_id=1, source_target_pairs={{0,2},{2,0},{1,3},{3,1},{4,6},{6,4},{5,7},{7,5},{8,10},{10,8},{9,1... | collective-permute-start | bytes 1572872 | tf_op jit(solution)/shard_map/ppermute | solution.py:39
  148.1 139.4 %collective-permute-start.16 = (bf16[512,1024]{1,0:T(8,128)(2,1)}, bf16[512,1024]{1,0:T(8,128)(2,1)}, u32[]{:S(2)}, u32[]{:S(2)}) collective-permute-start(bf16[512,1024]{1,0:T(8,128)(2,1)} %fusion.25.refs_0_), channel_id=1, source_target_pairs={{0,2},{2,0},{1,3},{3,1},{4,6},{6,4},{5,7},{7,5},{8,10},{10,8},{9,1... | collective-permute-start | bytes 3145736 | tf_op jit(solution)/shard_map/ppermute | solution.py:39
  230.3 43.1 %collective-permute-start.15 = (bf16[512,2048]{1,0:T(8,128)(2,1)}, bf16[512,2048]{1,0:T(8,128)(2,1)}, u32[]{:S(2)}, u32[]{:S(2)}) collective-permute-start(bf16[512,2048]{1,0:T(8,128)(2,1)} %get-tuple-element.178), channel_id=1, source_target_pairs={{0,2},{2,0},{1,3},{3,1},{4,6},{6,4},{5,7},{7,5},{8,10},{10,8},{9,1... | collective-permute-start | bytes 6291464 | tf_op jit(solution)/shard_map/ppermute | solution.py:39
  246.9 26.1 %collective-permute-start.14 = (bf16[512,1024]{1,0:T(8,128)(2,1)S(1)}, bf16[512,1024]{1,0:T(8,128)(2,1)}, u32[]{:S(2)}, u32[]{:S(2)}) collective-permute-start(bf16[512,1024]{1,0:T(8,128)(2,1)S(1)} %convert_element_type.128.refs_0_), channel_id=1, source_target_pairs={{0,2},{2,0},{1,3},{3,1},{4,6},{6,4},{5,7},{7,5},{8,10},{10,8},{9,1... | collective-permute-start | bytes 3145736 | tf_op jit(solution)/shard_map/ppermute | solution.py:39
  256.8 32.0 %collective-permute-start.17 = (bf16[512,2048]{1,0:T(8,128)(2,1)}, bf16[512,2048]{1,0:T(8,128)(2,1)}, u32[]{:S(2)}, u32[]{:S(2)}) collective-permute-start(bf16[512,2048]{1,0:T(8,128)(2,1)} %get-tuple-element.186), channel_id=1, source_target_pairs={{0,2},{2,0},{1,3},{3,1},{4,6},{6,4},{5,7},{7,5},{8,10},{10,8},{9,1... | collective-permute-start | bytes 6291464 | tf_op jit(solution)/shard_map/ppermute | solution.py:39
  273.1 48.7 %collective-permute-start.20 = (bf16[512,1024]{1,0:T(8,128)(2,1)S(1)}, bf16[512,1024]{1,0:T(8,128)(2,1)}, u32[]{:S(2)}, u32[]{:S(2)}) collective-permute-start(bf16[512,1024]{1,0:T(8,128)(2,1)S(1)} %convert_element_type.135.refs_2_), channel_id=1, source_target_pairs={{0,2},{2,0},{1,3},{3,1},{4,6},{6,4},{5,7},{7,5},{8,10},{10,8},{9,1... | collective-permute-start | bytes 3145736 | tf_op jit(solution)/shard_map/ppermute | solution.py:39
  286.0 50.4 %collective-permute-start.37 = (bf16[4,128,1024]{2,1,0:T(8,128)(2,1)}, bf16[4,128,1024]{2,1,0:T(8,128)(2,1)}, u32[]{:S(2)}, u32[]{:S(2)}) collective-permute-start(bf16[4,128,1024]{2,1,0:T(8,128)(2,1)} %get-tuple-element.97), channel_id=1, source_target_pairs={{0,1},{1,0},{2,3},{3,2},{4,5},{5,4},{6,7},{7,6},{8,9},{9,8},{10,11... | collective-permute-start | bytes 3145736 | tf_op jit(solution)/shard_map/ppermute | solution.py:39
  287.5 54.4 %collective-permute-start.38 = (bf16[2,2,128,1024]{3,2,1,0:T(8,128)(2,1)}, bf16[2,2,128,1024]{3,2,1,0:T(8,128)(2,1)}, u32[]{:S(2)}, u32[]{:S(2)}) collective-permute-start(bf16[2,2,128,1024]{3,2,1,0:T(8,128)(2,1)} %get-tuple-element.68.rest_0_), channel_id=1, source_target_pairs={{0,4},{4,0},{8,12},{12,8},{16,20},{20,16},{24,28},{28,24},{1,5},{5... | collective-permute-start | bytes 3145736 | tf_op jit(solution)/shard_map/ppermute | solution.py:43
  321.0 29.2 %collective-permute-start.31 = (bf16[2,2,128,1024]{3,2,1,0:T(8,128)(2,1)}, bf16[2,2,128,1024]{3,2,1,0:T(8,128)(2,1)S(1)}, u32[]{:S(2)}, u32[]{:S(2)}) collective-permute-start(bf16[2,2,128,1024]{3,2,1,0:T(8,128)(2,1)} %copy-done.14), channel_id=1, source_target_pairs={{0,4},{4,0},{8,12},{12,8},{16,20},{20,16},{24,28},{28,24},{1,5},{5... | collective-permute-start | bytes 3145736 | tf_op jit(solution)/shard_map/ppermute | solution.py:43
  321.8 27.2 %collective-permute-start.30 = (bf16[4,128,1024]{2,1,0:T(8,128)(2,1)}, bf16[4,128,1024]{2,1,0:T(8,128)(2,1)S(1)}, u32[]{:S(2)}, u32[]{:S(2)}) collective-permute-start(bf16[4,128,1024]{2,1,0:T(8,128)(2,1)} %copy-done.15), channel_id=1, source_target_pairs={{0,1},{1,0},{2,3},{3,2},{4,5},{5,4},{6,7},{7,6},{8,9},{9,8},{10,11... | collective-permute-start | bytes 3145736 | tf_op jit(solution)/shard_map/ppermute | solution.py:39
  335.0 39.3 %collective-permute-start.23 = (bf16[4,128,1024]{2,1,0:T(8,128)(2,1)S(1)}, bf16[4,128,1024]{2,1,0:T(8,128)(2,1)S(1)}, u32[]{:S(2)}, u32[]{:S(2)}) collective-permute-start(bf16[4,128,1024]{2,1,0:T(8,128)(2,1)S(1)} %get-tuple-element.74), channel_id=1, source_target_pairs={{0,1},{1,0},{2,3},{3,2},{4,5},{5,4},{6,7},{7,6},{8,9},{9,8},{10,11... | collective-permute-start | bytes 3145736 | tf_op jit(solution)/shard_map/ppermute | solution.py:39
  336.4 39.2 %collective-permute-start.24 = (bf16[2,2,128,1024]{3,2,1,0:T(8,128)(2,1)S(1)}, bf16[2,2,128,1024]{3,2,1,0:T(8,128)(2,1)S(1)}, u32[]{:S(2)}, u32[]{:S(2)}) collective-permute-start(bf16[2,2,128,1024]{3,2,1,0:T(8,128)(2,1)S(1)} %get-tuple-element.76), channel_id=1, source_target_pairs={{0,4},{4,0},{8,12},{12,8},{16,20},{20,16},{24,28},{28,24},{1,5},{5... | collective-permute-start | bytes 3145736 | tf_op jit(solution)/shard_map/ppermute | solution.py:43
  349.0 36.5 %collective-permute-start.39 = (bf16[2,128,1024]{2,1,0:T(8,128)(2,1)S(1)}, bf16[2,128,1024]{2,1,0:T(8,128)(2,1)S(1)}, u32[]{:S(2)}, u32[]{:S(2)}) collective-permute-start(bf16[2,128,1024]{2,1,0:T(8,128)(2,1)S(1)} %get-tuple-element.100), channel_id=1, source_target_pairs={{0,4},{4,0},{8,12},{12,8},{16,20},{20,16},{24,28},{28,24},{1,5},{5... | collective-permute-start | bytes 1572872 | tf_op jit(solution)/shard_map/ppermute | solution.py:43
  350.1 36.0 %collective-permute-start.40 = (bf16[2,128,1024]{2,1,0:T(8,128)(2,1)S(1)}, bf16[2,128,1024]{2,1,0:T(8,128)(2,1)S(1)}, u32[]{:S(2)}, u32[]{:S(2)}) collective-permute-start(bf16[2,128,1024]{2,1,0:T(8,128)(2,1)S(1)} %get-tuple-element.102), channel_id=1, source_target_pairs={{0,1},{1,0},{2,3},{3,2},{4,5},{5,4},{6,7},{7,6},{8,9},{9,8},{10,11... | collective-permute-start | bytes 1572872 | tf_op jit(solution)/shard_map/ppermute | solution.py:39
  352.8 35.4 %collective-permute-start.18 = (bf16[256,1024]{1,0:T(8,128)(2,1)S(1)}, bf16[256,1024]{1,0:T(8,128)(2,1)S(1)}, u32[]{:S(2)}, u32[]{:S(2)}) collective-permute-start(bf16[256,1024]{1,0:T(8,128)(2,1)S(1)} %get-tuple-element.145), channel_id=1, source_target_pairs={{0,2},{2,0},{1,3},{3,1},{4,6},{6,4},{5,7},{7,5},{8,10},{10,8},{9,1... | collective-permute-start | bytes 1572872 | tf_op jit(solution)/shard_map/ppermute | solution.py:39
  375.6 24.1 %collective-permute-start.33 = (bf16[2,128,1024]{2,1,0:T(8,128)(2,1)S(1)}, bf16[2,128,1024]{2,1,0:T(8,128)(2,1)S(1)}, u32[]{:S(2)}, u32[]{:S(2)}) collective-permute-start(bf16[2,128,1024]{2,1,0:T(8,128)(2,1)S(1)} %get-tuple-element.91), channel_id=1, source_target_pairs={{0,1},{1,0},{2,3},{3,2},{4,5},{5,4},{6,7},{7,6},{8,9},{9,8},{10,11... | collective-permute-start | bytes 1572872 | tf_op jit(solution)/shard_map/ppermute | solution.py:39
  385.5 32.0 %collective-permute-start.25 = (bf16[2,128,1024]{2,1,0:T(8,128)(2,1)S(1)}, bf16[2,128,1024]{2,1,0:T(8,128)(2,1)S(1)}, u32[]{:S(2)}, u32[]{:S(2)}) collective-permute-start(bf16[2,128,1024]{2,1,0:T(8,128)(2,1)S(1)} %get-tuple-element.78), channel_id=1, source_target_pairs={{0,4},{4,0},{8,12},{12,8},{16,20},{20,16},{24,28},{28,24},{1,5},{5... | collective-permute-start | bytes 1572872 | tf_op jit(solution)/shard_map/ppermute | solution.py:43
  386.2 32.5 %collective-permute-start.26 = (bf16[2,128,1024]{2,1,0:T(8,128)(2,1)S(1)}, bf16[2,128,1024]{2,1,0:T(8,128)(2,1)S(1)}, u32[]{:S(2)}, u32[]{:S(2)}) collective-permute-start(bf16[2,128,1024]{2,1,0:T(8,128)(2,1)S(1)} %get-tuple-element.80), channel_id=1, source_target_pairs={{0,1},{1,0},{2,3},{3,2},{4,5},{5,4},{6,7},{7,6},{8,9},{9,8},{10,11... | collective-permute-start | bytes 1572872 | tf_op jit(solution)/shard_map/ppermute | solution.py:39
  401.9 63.4 %collective-permute-start.13 = (bf16[2,256,1024]{2,1,0:T(8,128)(2,1)S(1)}, bf16[2,256,1024]{2,1,0:T(8,128)(2,1)}, u32[]{:S(2)}, u32[]{:S(2)}) collective-permute-start(bf16[2,256,1024]{2,1,0:T(8,128)(2,1)S(1)} %maximum_select_fusion.3), channel_id=1, source_target_pairs={{0,1},{1,0},{2,3},{3,2},{4,5},{5,4},{6,7},{7,6},{8,9},{9,8},{10,11... | collective-permute-start | bytes 3145736 | tf_op jit(solution)/shard_map/ppermute | solution.py:39
  416.8 51.8 %collective-permute-start.19 = (bf16[2,256,1024]{2,1,0:T(8,128)(2,1)S(1)}, bf16[2,256,1024]{2,1,0:T(8,128)(2,1)}, u32[]{:S(2)}, u32[]{:S(2)}) collective-permute-start(bf16[2,256,1024]{2,1,0:T(8,128)(2,1)S(1)} %maximum_select_fusion.4), channel_id=1, source_target_pairs={{0,1},{1,0},{2,3},{3,2},{4,5},{5,4},{6,7},{7,6},{8,9},{9,8},{10,11... | collective-permute-start | bytes 3145736 | tf_op jit(solution)/shard_map/ppermute | solution.py:39
  417.4 33.8 %collective-permute-start.35 = (bf16[128,1024]{1,0:T(8,128)(2,1)S(1)}, bf16[128,1024]{1,0:T(8,128)(2,1)S(1)}, u32[]{:S(2)}, u32[]{:S(2)}) collective-permute-start(bf16[128,1024]{1,0:T(8,128)(2,1)S(1)} %get-tuple-element.94), channel_id=1, source_target_pairs={{0,16},{4,20},{8,24},{12,28},{16,0},{20,4},{24,8},{28,12},{1,17},{... | collective-permute-start | bytes 786440 | tf_op jit(solution)/shard_map/ppermute | solution.py:47
  418.7 32.5 %collective-permute-start.34 = (bf16[128,1024]{1,0:T(8,128)(2,1)S(1)}, bf16[128,1024]{1,0:T(8,128)(2,1)S(1)}, u32[]{:S(2)}, u32[]{:S(2)}) collective-permute-start(bf16[128,1024]{1,0:T(8,128)(2,1)S(1)} %get-tuple-element.93), channel_id=1, source_target_pairs={{0,8},{4,12},{8,16},{12,20},{16,24},{20,28},{24,0},{28,4},{1,9},{5... | collective-permute-start | bytes 786440 | tf_op jit(solution)/shard_map/ppermute | solution.py:47
  424.3 27.3 %collective-permute-start.29 = (bf16[128,1024]{1,0:T(8,128)(2,1)S(1)}, bf16[128,1024]{1,0:T(8,128)(2,1)S(1)}, u32[]{:S(2)}, u32[]{:S(2)}) collective-permute-start(bf16[128,1024]{1,0:T(8,128)(2,1)S(1)} %get-tuple-element.84), channel_id=1, source_target_pairs={{0,24},{4,28},{8,0},{12,4},{16,8},{20,12},{24,16},{28,20},{1,25},{... | collective-permute-start | bytes 786440 | tf_op jit(solution)/shard_map/ppermute | solution.py:47
  (79 other events, 672.3 us)
Sparse Core Ops, SparseCore 0:
  10.9 138.3 all-gather.2
  321.1 57.5 all-gather.4
